TPU v7x, 32 devices: a whole 2x2x4 slice. The times are simulated.
32 devices in a mesh: dp: 8 (over z, x), row: 2 (over y), col: 2 (over core).
Axes of the slice: x: 2, y: 2, z: 4, core: 2. Of those that a mesh axis runs over, the one named last changes fastest.
Arguments:
- inputs: bfloat16 [4096, 2048], P('dp', ('col', 'row')), may hold values from -6 to 6
- norm_gain: bfloat16 [2048], P(('col', 'row')), may hold values from 0.5 to 1.5
- norm_shift: bfloat16 [2048], P(('col', 'row')), may hold values from -3 to 3
- qkv_weight: bfloat16 [2048, 6144], P('col', 'row'), may hold values from -0.125 to 0.125
- qkv_bias: bfloat16 [6144], P(('row', 'col')), may hold values from -3 to 3
- up_weight: bfloat16 [2048, 8192], P('col', 'row')
- up_bias: bfloat16 [8192], P(('row', 'col')), may hold values from -3 to 3
- dense_weight: bfloat16 [2048, 2048], P('row', 'col'), may hold values from -0.75 to 0.75
- down_weight: bfloat16 [8192, 2048], P('row', 'col'), may hold values from -0.0625 to 0.0625
- out_bias: bfloat16 [2048], P(('col', 'row')), may hold values from -3 to 3
- cotangent: bfloat16 [4096, 2048], P('dp', ('col', 'row')), may hold values from -6 to 6
- seq_lengths: int32 [32], replicated, may hold values from 1 to 512, as said below
- seq_owner: int32 [32], replicated, may hold values from 0 to 7, as said below
Outputs:
- outputs: bfloat16 [4096, 2048], P('dp', ('col', 'row'))
- grad_inputs: float32 [4096, 2048], P('dp', ('col', 'row'))
- grad_norm_gain: float32 [2048], P(('col', 'row'))
- grad_norm_shift: float32 [2048], P(('col', 'row'))
- grad_qkv_weight: float32 [2048, 6144], P(('col', 'dp'), 'row')
- grad_qkv_bias: float32 [6144], P(('row', 'col'))
- grad_up_weight: float32 [2048, 8192], P(('col', 'dp'), 'row')
- grad_up_bias: float32 [8192], P(('row', 'col'))
- grad_dense_weight: float32 [2048, 2048], P(('row', 'dp'), 'col')
- grad_down_weight: float32 [8192, 2048], P(('row', 'dp'), 'col')
- grad_out_bias: float32 [2048], P(('col', 'row'))
Inputs may be any that keep to these rules, and one draw needn't show every extreme that they name: `seq_lengths`: the lengths of the sequences held by one index of dp sum to at most 512; in every draw one sequence is 512 long and is the only one of its index. `seq_owner`: loads differ between indices of dp; an index may hold no sequence.
All inputs are finite; a program needn't handle non-finite values.
Results may differ from a plain program's by a relative error of at most 0.0097.
Values may be sent and summed in bfloat16 or wider, within the bound.
A program may use at most 256 MiB of HBM per device.

v0:
```python
from functools import partial
import math

import jax
import jax.numpy as jnp
import numpy as np
from jax import lax
from jax.experimental import pallas as pl
from jax.experimental.pallas import tpu as pltpu
from jax.sharding import PartitionSpec as P

HEAD_DIM = 64
ROT = 32
HALF_ROT = ROT // 2
PAIR = 2 * HEAD_DIM
PAIR_QKV = 3 * PAIR

epsilon = 1e-05
masked_score = -1e30
rope_base = 10000.0
VMEM_LIMIT = 67_000_000
SCRATCH_LIMIT = 58 * 1024 * 1024
SENDS = 48
score_scale = HEAD_DIM ** (-0.5)
bf16 = jnp.bfloat16
f32 = jnp.float32


def layout(seq_lengths, seq_owner, device, row_count):
    owned = seq_owner == device
    lengths_owned = jnp.where(owned, seq_lengths, 0)
    seq_ends = jnp.cumsum(lengths_owned, dtype=jnp.int32)
    seq_starts = seq_ends - lengths_owned
    slot_index = jnp.arange(row_count, dtype=jnp.int32)
    segment = jnp.sum((seq_ends[None, :] <= slot_index[:, None]).astype(jnp.int32), axis=1)
    picked = jnp.arange(seq_lengths.shape[0], dtype=jnp.int32)[None, :] == segment[:, None]
    seq_begin = jnp.sum(jnp.where(picked, seq_starts[None, :], 0), axis=1)
    position = slot_index - seq_begin
    is_valid = slot_index < seq_ends[-1]
    return (segment, position, is_valid)


def rotation_tables(position):
    index_range = jnp.arange(HALF_ROT, dtype=f32)
    frequency = rope_base ** (-2.0 * index_range / ROT)
    phase = position.astype(f32)[:, None] * frequency[None, :]
    cosines, sines = jnp.cos(phase), jnp.sin(phase)
    rows = position.shape[0]
    ones = jnp.ones((rows, HEAD_DIM - ROT), f32)
    none = jnp.zeros((rows, HALF_ROT), f32)
    rest = jnp.zeros((rows, HEAD_DIM - ROT), f32)
    same = jnp.concatenate([cosines, cosines, ones], axis=1)
    from_right = jnp.concatenate([sines, none, rest], axis=1)
    from_left = jnp.concatenate([none, sines, rest], axis=1)
    return jnp.stack([same, from_right, from_left])


def turned(array):
    return jnp.swapaxes(array, 0, 1)


def contract(left, right, left_dim, right_dim):
    dims = (((left_dim,), (right_dim,)), ((), ()))
    return lax.dot_general(left, right, dims, preferred_element_type=f32)


gelu_rate = math.sqrt(2.0 / math.pi)
gelu_cube = 0.044715


def gelu(x):
    return 0.5 * x * (1.0 + jnp.tanh(gelu_rate * (x + gelu_cube * x * x * x)))


def gelu_slope(x):
    square = x * x
    bent = jnp.tanh(gelu_rate * (x + gelu_cube * x * square))
    return 0.5 * (1.0 + bent) + 0.5 * x * (1.0 - bent * bent) * (gelu_rate * (1.0 + 3.0 * gelu_cube * square))


def attention_pair(proj, mixed, tables, seg_col, seg_row):
    rows = proj.shape[0]
    block = min(256, rows)
    same, from_right, from_left = tables[0], tables[1], tables[2]

    def rotate(part, sign):
        right = jnp.concatenate([part[:, HALF_ROT:], part[:, :HALF_ROT]], axis=1)
        left = jnp.concatenate([part[:, HEAD_DIM - HALF_ROT :], part[:, : HEAD_DIM - HALF_ROT]], axis=1)
        return part * same - sign * (right * from_right) + sign * (left * from_left)

    attended_heads, grads = [], []
    for head in range(2):
        base = head * 3 * HEAD_DIM
        queries = rotate(proj[:, base : base + HEAD_DIM], 1.0).astype(bf16)
        keys = rotate(proj[:, base + HEAD_DIM : base + 2 * HEAD_DIM], 1.0).astype(bf16)
        values = proj[:, base + 2 * HEAD_DIM : base + 3 * HEAD_DIM].astype(bf16)
        d_outs = mixed[:, head * HEAD_DIM : (head + 1) * HEAD_DIM]
        outs, d_queries, d_keys, d_values = [], [], None, None
        for first in range(0, rows, block):
            last = first + block
            q, d_out = queries[first:last], d_outs[first:last]
            k, v = keys[:last], values[:last]
            row_index = first + lax.broadcasted_iota(jnp.int32, (block, last), 0)
            key_index = lax.broadcasted_iota(jnp.int32, (block, last), 1)
            allowed = (seg_col[first:last, :] == seg_row[:, :last]) & (key_index <= row_index)
            scores = jnp.where(allowed, contract(q, k, 1, 1) * score_scale, masked_score)
            weights = jnp.exp(scores - jnp.max(scores, axis=1, keepdims=True))
            probs = weights * (1.0 / jnp.sum(weights, axis=1, keepdims=True))
            probs_low = probs.astype(bf16)
            outs.append(contract(probs_low, v, 1, 0))
            d_probs = contract(d_out, v, 1, 1)
            row_dot = jnp.sum(probs * d_probs, axis=1, keepdims=True)
            d_scores = (probs * (d_probs - row_dot)).astype(bf16)
            d_queries.append(contract(d_scores, k, 1, 0))
            key_part = contract(d_scores, q, 0, 0)
            value_part = contract(probs_low, d_out, 0, 0)
            if d_keys is None:
                d_keys, d_values = key_part, value_part
            else:
                d_keys = jnp.concatenate([key_part[:first] + d_keys, key_part[first:]], axis=0)
                d_values = jnp.concatenate([value_part[:first] + d_values, value_part[first:]], axis=0)
        attended_heads.append(jnp.concatenate(outs, axis=0))
        grads.append(rotate(jnp.concatenate(d_queries, axis=0) * score_scale, -1.0))
        grads.append(rotate(d_keys * score_scale, -1.0))
        grads.append(d_values)
    attended = jnp.concatenate(attended_heads, axis=1).astype(bf16)
    return attended, jnp.concatenate(grads, axis=1).astype(bf16)


class Sizes:
    def __init__(self, dp_size, inputs, qkv_weight, up_weight, dense_weight, down_weight, seq_lengths):
        self.dp = dp_size
        self.seqs = seq_lengths.shape[0]
        self.line = dp_size // 2
        self.rows, self.quarter = inputs.shape
        self.half = up_weight.shape[0]
        self.width = 2 * self.half
        self.up_chunk = self.half // dp_size
        self.down_chunk = down_weight.shape[0] // dp_size
        self.dense_chunk = dense_weight.shape[0] // dp_size
        self.hidden = up_weight.shape[1] // 2
        self.tiles = self.hidden // self.down_chunk
        self.qkv = qkv_weight.shape[1] // 2
        self.pairs = self.qkv // PAIR_QKV
        self.features = dense_weight.shape[0] // 2


def flows_of(z):
    return dict(
        down=(z.down_chunk // z.up_chunk, z.up_chunk, z.quarter),
        up=(z.tiles, z.up_chunk, z.down_chunk),
        dense=(1, z.dense_chunk, z.quarter),
        qkv=(z.pairs, z.up_chunk, PAIR_QKV),
    )


def scratch_of(z):
    rows, q, line, tiles, pairs = z.rows, z.quarter, z.line, z.tiles, z.pairs
    up, down, dense = z.up_chunk, z.down_chunk, z.dense_chunk
    shapes = dict(
        inq=((2, 2, rows, q), bf16),
        cotq=((2, 2, rows, q), bf16),
        cotp=((2, rows, q), bf16),
        gainq=((2, 2, 16, q), f32),
        seg_col=((rows, 1), f32),
        seg_row=((1, rows), f32),
        tables=((3, rows, HEAD_DIM), f32),
        up_b=((tiles, 1, down), f32),
        qkv_b=((pairs, 1, PAIR_QKV), f32),
        sums=((1, 3 * q + z.qkv + z.hidden), f32),
        sums_got=((3, 1, 3 * q + z.qkv + z.hidden), f32),
        sums_send=((2, 1, 3 * q + z.qkv + z.hidden), f32),
        hid=((2, rows, z.half), bf16),
        hid_own=((line, rows, up), bf16),
        hid_send=((line, rows, up), bf16),
        hid_pair=((line, rows, up), bf16),
        stat=((2, rows, 1), f32),
        before=((tiles, rows, down), f32),
        act=((tiles, rows, down), bf16),
        act_own=((line, rows, down), bf16),
        act_pair=((line, rows, down), bf16),
        db_mine=((tiles, rows, down), bf16),
        db_theirs=((tiles, rows, down), bf16),
        db_mine_pair=((tiles, rows, down), bf16),
        db_theirs_pair=((tiles, rows, down), bf16),
        mixed=((pairs, rows, PAIR), bf16),
        att=((rows, z.features), bf16),
        att_part=((line, rows, dense), bf16),
        att_own=((line, rows, dense), bf16),
        att_pair=((line, rows, dense), bf16),
        dp_mine=((pairs, rows, PAIR_QKV), bf16),
        dp_theirs=((pairs, rows, PAIR_QKV), bf16),
        dp_mine_pair=((pairs, rows, PAIR_QKV), bf16),
        dp_theirs_pair=((pairs, rows, PAIR_QKV), bf16),
        weight=((2, 2, z.half, 512), bf16),
        st_down=((line, 2) + flows_of(z)["down"], bf16),
        st_up=((line, 2) + flows_of(z)["up"], bf16),
        st_dense=((line, 2) + flows_of(z)["dense"], bf16),
        st_qkv=((line, 2) + flows_of(z)["qkv"], bf16),
        got_down=(flows_of(z)["down"], bf16),
        got_up=(flows_of(z)["up"], bf16),
        got_dense=(flows_of(z)["dense"], bf16),
        got_qkv=(flows_of(z)["qkv"], bf16),
        part_send=((2, rows, q), bf16),
        part_row=((rows, q), bf16),
        out_row=((rows, q), bf16),
        dh_row=((rows, q), bf16),
        sum_send=((2, 8, rows), f32),
        sum_got=((2, 8, rows), f32),
    )
    if shapes["before"][0] != (4, rows, q):
        shapes["total"] = ((4, rows, q), f32)
    if shapes["st_up"] == shapes["st_down"]:
        del shapes["st_up"], shapes["got_up"]
    return shapes


def fits(z):
    total = 0
    for shape, kind in scratch_of(z).values():
        total += math.prod(shape[:-1]) * -(-shape[-1] // 128) * 128 * jnp.dtype(kind).itemsize
    return z.line >= 4 and z.line % 2 == 0 and total <= SCRATCH_LIMIT


def layer_kernel(z, names, *refs):
    r = dict(zip(names, refs))
    rows, q, line, tiles, pairs = z.rows, z.quarter, z.line, z.tiles, z.pairs
    half_line = line // 2
    if "total" not in r:
        r["total"] = r["before"]
    r["dh_got"], r["out_got"] = r["inq"].at[1], r["cotq"].at[1]
    shared = "st_up" not in r
    if shared:
        r["st_up"], r["got_up"] = r["st_down"], r["got_down"]
    dp = lax.axis_index("dp")
    row = lax.axis_index("row")
    col = lax.axis_index("col")
    place, side = dp // 2, lax.rem(dp, 2)
    other_row, other_col, other_side = 1 - row, 1 - col, 1 - side
    to_row = {"row": other_row}
    to_col = {"col": other_col}
    to_side = {"dp": dp + 1 - 2 * side}
    MESH = pl.DeviceIdType.MESH

    marks = dict(send=0, recv=0, local=0)

    def take(kind, count):
        first = marks[kind]
        marks[kind] += count
        return first

    def remote(src, dst, send, recv, device):
        return pltpu.make_async_remote_copy(
            src_ref=src,
            dst_ref=dst,
            send_sem=r["send_sem"].at[send],
            recv_sem=r["recv_sem"].at[recv],
            device_id=device,
            device_id_type=MESH,
        )

    pending = []

    class Message:
        def __init__(self, src, dst, device, got=None):
            index = (take("send", 1), take("recv", 1))
            self.copy = lambda: remote(src, dst, *index, device)
            self.got = lambda: remote(src if got is None else got, dst if got is None else got, *index, device)

        def start(self):
            self.copy().start()
            pending.append(self)

        def wait(self):
            self.got().wait_recv()

    right, left = {"dp": dp + 2}, {"dp": dp - 2}
    has_right, has_left = place < line - 1, place > 0
    at_end, near_end = (place == 0) | (place == line - 1), (place == 1) | (place == line - 2)
    inward, outward = {"dp": dp + 2 - 4 * (place > 0)}, {"dp": dp + 2 - 4 * (place == 1)}
    barrier = pltpu.get_barrier_semaphore()
    for device in (to_row, to_col, to_side):
        pl.semaphore_signal(barrier, inc=1, device_id=device, device_id_type=MESH)

    @pl.when(has_right)
    def _():
        pl.semaphore_signal(barrier, inc=1, device_id=right, device_id_type=MESH)

    @pl.when(has_left)
    def _():
        pl.semaphore_signal(barrier, inc=1, device_id=left, device_id_type=MESH)

    slots = lax.broadcasted_iota(jnp.int32, (8, rows), 1)

    def add_sequence(number, carry):
        end, segments, begins = carry
        start = end
        end = start + jnp.where(r["seq_owner"][number] == dp, r["seq_lengths"][number], 0)
        segments = segments + (end <= slots).astype(jnp.int32)
        begins = jnp.where((start <= slots) & (slots < end), start, begins)
        return end, segments, begins

    nothing = jnp.zeros((8, rows), jnp.int32)
    segments, begins = lax.fori_loop(0, z.seqs, add_sequence, (jnp.int32(0), nothing, nothing))[1:]
    segments = segments.astype(f32)
    r["seg_row"][...] = segments[:1]
    r["seg_col"][...] = turned(segments)[:, :1]
    cot = r["cot"]
    valid = (r["seg_col"][...] < z.seqs).astype(f32)
    r["cotq"][0, row] = cot[...] * valid.astype(bf16)

    def as_row(vector):
        return vector.astype(f32).reshape(1, vector.shape[0])

    r["gainq"][0, row] = jnp.concatenate(
        [
            jnp.broadcast_to(as_row(r["norm_gain"][...]), (8, q)),
            jnp.broadcast_to(as_row(r["norm_shift"][...]), (8, q)),
        ]
    )
    pl.semaphore_wait(barrier, 3 + has_right.astype(jnp.int32) + has_left.astype(jnp.int32))

    def gather(src, held):
        over = Message(src, held.at[0, row], to_row, held.at[0, other_row])
        across = Message(src, held.at[1, row], to_col, held.at[1, row])
        onward = Message(held.at[0, other_row], held.at[1, other_row], to_col, held.at[1, other_row])
        return over, across, onward

    in_over, in_across, in_onward = gather(r["inputs"], r["inq"])
    gain_over, gain_across, gain_onward = gather(r["gainq"].at[0, row], r["gainq"])
    cot_over, cot_across, cot_onward = gather(r["cotq"].at[0, row], r["cotq"])
    cot_side = Message(r["cotq"].at[0, row], r["cotp"].at[row], to_side)
    cot_side_onward = Message(r["cotq"].at[0, other_row], r["cotp"].at[other_row], to_side)
    hid_side = Message(r["hid_send"], r["hid_pair"], to_side)

    end_cot_send, end_cot_recv = take("send", 4), take("recv", 4)

    def end_cot(pair, part, device):
        src = r["cotp"].at[part] if pair else r["cotq"].at[0, part]
        index = 2 * pair + part
        return remote(src, r["end_cot"].at[pair, part], end_cot_send + index, end_cot_recv + index, device)

    def send_end_cot(pair, part):
        @pl.when(at_end)
        def _():
            end_cot(pair, part, inward).start()

    def loop(first, last, work):
        def one(k, carry):
            work(k)
            return carry

        lax.fori_loop(first, last, one, 0)

    def pass_on(got, onward):
        def work(k):
            got(k).wait_recv()
            onward(k).start()

        return work

    def waits(*copies):
        def work(k):
            for copy in copies:
                copy(k).wait_recv()

        return work

    class EndRows:
        def __init__(self, own, pair, land):
            self.own, self.pair, self.land = own, pair, land
            self.send, self.recv = take("send", line), take("recv", line)
            self.on_send, self.on_recv = take("send", line), take("recv", line)

        def copy(self, chunk, device, pair):
            src = (self.pair if pair else self.own).at[chunk]
            return remote(src, self.land.at[chunk, int(pair)], self.send + chunk, self.recv + chunk, device)

        def onward(self, chunk):
            part = self.land.at[chunk, col]
            return remote(part, part, self.on_send + chunk, self.on_recv + chunk, to_col)

        def start(self, pair, first, last):
            kind = 1 if pair else 0

            @pl.when(at_end & (col == kind))
            def _():
                def one(number):
                    chunk = jnp.where(place == 0, line - 1 - number, number)
                    self.copy(chunk, inward, pair).start()

                loop(first, last, one)

        def bring(self, chunk):
            self.copy(chunk, outward, False).wait_recv()
            self.onward(chunk).start()
            self.onward(chunk).wait_recv()

        def finish(self):
            def one(chunk):
                @pl.when(at_end & (chunk != place))
                def _():
                    self.copy(chunk, inward, False).wait_send()

                @pl.when(near_end)
                def _():
                    gone = jnp.where(place == 1, 0, line - 1)

                    @pl.when(chunk != gone)
                    def _():
                        self.onward(chunk).wait_send()

            loop(0, line, one)

    end_act = EndRows(r["act_own"], r["act_pair"], r["end_act"])
    end_att = EndRows(r["att_own"], r["att_pair"], r["end_att"])
    swaps = {
        "up": Message(r["up_w"].at[:, pl.ds(pl.multiple_of(other_col * z.hidden, 128), z.hidden)], r["up_o"], to_col, r["up_o"]),
        "qkv": Message(r["qkv_w"].at[:, pl.ds(pl.multiple_of(other_col * z.qkv, 128), z.qkv)], r["qkv_o"], to_col, r["qkv_o"]),
        "down": Message(r["down_w"].at[pl.ds(pl.multiple_of(other_col * z.hidden, 16), z.hidden), :], r["down_o"], to_col, r["down_o"]),
        "dense": Message(r["dense_w"].at[pl.ds(pl.multiple_of(other_col * z.features, 16), z.features), :], r["dense_o"], to_col, r["dense_o"]),
    }

    def local(src, dst, index):
        return pltpu.make_async_copy(src, dst, r["local_sem"].at[index])

    stream_base = take("local", 8)
    once = take("local", 4)

    in_over.start()
    gain_over.start()
    in_across.start()
    gain_across.start()
    keep_in = local(r["inputs"], r["inq"].at[0, row], once)
    keep_in.start()
    cot_side.start()
    send_end_cot(0, row)
    swaps["up"].start()
    up_bias, qkv_bias = as_row(r["up_bias"][...]), as_row(r["qkv_bias"][...])
    for tile in range(tiles):
        r["up_b"][tile] = up_bias[:, tile * z.down_chunk : (tile + 1) * z.down_chunk]
    for pair in range(pairs):
        r["qkv_b"][pair] = qkv_bias[:, pair * PAIR_QKV : (pair + 1) * PAIR_QKV]
    position = turned((slots - begins).astype(f32))[:, :1]
    phase = position * r["frequency"][...]
    lane = lax.broadcasted_iota(jnp.int32, (1, HEAD_DIM), 1)
    sines = jnp.sin(phase)
    r["tables"][0] = jnp.where(lane < ROT, jnp.cos(phase), 1.0)
    r["tables"][1] = jnp.where(lane < HALF_ROT, sines, 0.0)
    r["tables"][2] = jnp.where((lane >= HALF_ROT) & (lane < ROT), sines, 0.0)
    gain_over.wait()
    gain_onward.start()
    in_over.wait()
    in_onward.start()
    cot_over.start()
    cot_across.start()
    cot_side.wait()
    send_end_cot(1, row)
    keep_in.wait()
    gain_across.wait()
    gain_onward.wait()
    in_across.wait()
    in_onward.wait()

    block = min(64, rows)

    def norm_rows(step, carry):
        at = pl.ds(pl.multiple_of(step * block, block), block)
        parts = [r["inq"][h, p, at].astype(f32) for h in range(2) for p in range(2)]
        total = parts[0] + parts[1] + parts[2] + parts[3]
        squares = parts[0] * parts[0] + parts[1] * parts[1] + parts[2] * parts[2] + parts[3] * parts[3]
        average = jnp.sum(total, axis=1, keepdims=True) / z.width
        variance = jnp.sum(squares, axis=1, keepdims=True) / z.width - average * average
        scale_inv = lax.rsqrt(variance + epsilon)
        r["stat"][0, at] = average
        r["stat"][1, at] = scale_inv
        for h in range(2):
            for p in range(2):
                normed = (parts[2 * h + p] - average) * scale_inv
                gain, shift = r["gainq"][h, p, 0:1, :], r["gainq"][h, p, 8:9, :]
                r["hid"][h, at, p * q : (p + 1) * q] = (normed * gain + shift).astype(bf16)
        return carry

    lax.fori_loop(0, rows // block, norm_rows, 0)
    for c in range(line):
        even = r["hid"][0, :, 2 * c * z.up_chunk : (2 * c + 1) * z.up_chunk]
        odd = r["hid"][0, :, (2 * c + 1) * z.up_chunk : (2 * c + 2) * z.up_chunk]
        r["hid_own"][c] = jnp.where(side == 0, even, odd)
        r["hid_send"][c] = jnp.where(side == 0, odd, even)

    def stream(count, copies, work):
        for copy in copies(jnp.int32(0), jnp.int32(0)):
            copy.start()

        def one(step, carry):
            slot = lax.rem(step, 2)

            @pl.when(step + 1 < count)
            def _():
                for copy in copies(step + 1, 1 - slot):
                    copy.start()

            for copy in copies(step, slot):
                copy.wait()
            work(step, slot)
            return carry

        lax.fori_loop(0, count, one, 0)

    def column_tiles(name, each, tile_of=lambda step: step):
        def copies(step, slot):
            tile = tile_of(step)
            mine = r[name + "_w"].at[:, pl.ds(pl.multiple_of((col * r[name + "_o"].shape[1]) + tile * each, 128), each)]
            theirs = r[name + "_o"].at[:, pl.ds(pl.multiple_of(tile * each, 128), each)]
            return [
                local(mine, r["weight"].at[slot, 0, :, :each], stream_base + slot * 4),
                local(theirs, r["weight"].at[slot, 1, :, :each], stream_base + slot * 4 + 1),
            ]

        return copies

    def row_tiles(name, each, tile_of=lambda step: step):
        def copies(step, slot):
            tile = tile_of(step)
            found = []
            for h in range(2):
                start = tile * each + (col * r[name + "_o"].shape[0] if h == 0 else 0)
                src = r[name + ("_w" if h == 0 else "_o")]
                for p in range(2):
                    found.append(
                        local(
                            src.at[pl.ds(pl.multiple_of(start, 16), each), p * q : (p + 1) * q],
                            r["weight"].at[slot, h, p * q : p * q + each, :],
                            stream_base + slot * 4 + 2 * h + p,
                        )
                    )
            return found

        return copies

    def rank_of(j):
        return jnp.where(col == 1, half_line - 1 - j, j)

    def tile_at(step):
        later = (step >= half_line).astype(jnp.int32)
        return 2 * rank_of(step - later * half_line) + jnp.where(later == 1, side, other_side)

    act_side_send, act_side_recv = take("send", half_line), take("recv", half_line)
    act_col_send, act_col_recv = take("send", half_line), take("recv", half_line)
    act_on_send, act_on_recv = take("send", half_line), take("recv", half_line)

    def act_side(j):
        tile, slot = 2 * rank_of(j) + other_side, col * half_line + rank_of(j)
        return remote(r["act"].at[tile], r["act_pair"].at[slot], act_side_send + j, act_side_recv + j, to_side)

    def act_col(j):
        slot = col * half_line + rank_of(j)
        return remote(r["act_own"].at[slot], r["act_own"].at[slot], act_col_send + j, act_col_recv + j, to_col)

    def act_on(j):
        slot = col * half_line + rank_of(j)
        return remote(r["act_pair"].at[slot], r["act_pair"].at[slot], act_on_send + j, act_on_recv + j, to_col)

    def up_work(step, slot):
        tile = tile_at(step)
        before = contract(r["hid"][0], r["weight"][slot, 0, :, : z.down_chunk], 1, 0)
        before = before + contract(r["hid"][1], r["weight"][slot, 1, :, : z.down_chunk], 1, 0)
        before = before + r["up_b"][tile]
        r["before"][tile] = before
        activated = gelu(before).astype(bf16)
        r["act"][tile] = activated

        @pl.when(step < half_line)
        def _():
            act_side(step).start()

        @pl.when(step >= half_line)
        def _():
            j = step - half_line
            r["act_own"][col * half_line + rank_of(j)] = activated
            act_col(j).start()

    hid_side.start()
    swaps["down"].start()
    swaps["up"].wait()
    stream(tiles, column_tiles("up", z.down_chunk, tile_at), up_work)

    cot_over.wait()
    cot_onward.start()
    cot_side_onward.start()
    send_end_cot(0, other_row)
    loop(0, half_line, waits(act_col))
    end_act.start(False, 0, line - 1)
    swaps["qkv"].start()
    swaps["dense"].start()
    cot_across.wait()
    cot_onward.wait()
    swaps["down"].wait()

    def each_side(name, count):
        side_send, side_recv = take("send", count), take("recv", count)
        col_send, col_recv = take("send", count), take("recv", count)
        on_send, on_recv = take("send", count), take("recv", count)
        mine, theirs = r[name + "_mine"], r[name + "_theirs"]
        mine_pair, theirs_pair = r[name + "_mine_pair"], r[name + "_theirs_pair"]

        def to_side_peer(k):
            return remote(mine.at[k], mine_pair.at[k], side_send + k, side_recv + k, to_side)

        def to_col_peer(k):
            return remote(mine.at[k], theirs.at[k], col_send + k, col_recv + k, to_col)

        def onward(k):
            return remote(mine_pair.at[k], theirs_pair.at[k], on_send + k, on_recv + k, to_col)

        return to_side_peer, to_col_peer, onward

    db_side, db_col, db_on = each_side("db", tiles)
    dp_side, dp_col, dp_on = each_side("dp", pairs)

    def over_weight_rows(slot, each, lefts):
        total = None
        for h in range(2):
            for p in range(2):
                part = contract(lefts(h, p), r["weight"][slot, h, p * q : p * q + each, :], 1, 1)
                total = part if total is None else total + part
        return total

    def down_work(step, slot):
        tile = step
        d_activated = over_weight_rows(slot, z.down_chunk, lambda h, p: r["cotq"][h, p])
        d_before = (d_activated * gelu_slope(r["before"][tile])).astype(bf16)
        r["db_mine"][tile] = d_before
        sums = jnp.sum(d_before.astype(f32), axis=0, keepdims=True)
        r["sums"][:, pl.ds(pl.multiple_of(2 * q + z.qkv + tile * z.down_chunk, 128), z.down_chunk)] = sums
        db_col(tile).start()
        db_side(tile).start()

    stream(tiles, row_tiles("down", z.down_chunk), down_work)

    class Flow:
        def __init__(self, name, own_rows, pair_rows, own_columns, pair_columns, split=False, by_col=False, earlier=None, ends=None):
            self.name, self.split, self.by_col, self.earlier, self.ends = name, split, by_col, earlier, ends
            self.own_rows, self.pair_rows = own_rows, pair_rows
            self.own_columns, self.pair_columns = own_columns, pair_columns
            self.stage, self.land, self.got = r["st_" + name], r["land_" + name], r["got_" + name]
            self.count, self.depth = flows_of(z)[name][:2]
            self.send = take("send", 2 * line)
            self.recv = take("recv", 2 * (line + 2))
            self.local = take("local", 1)
            self.later = False

        def half(self, group):
            return jnp.where(col == 0, group, 1 - group) if self.by_col else group

        def copy(self, chunk, group, slot, device):
            half = self.half(group)
            return remote(
                self.stage.at[chunk, half],
                self.land.at[slot, half],
                self.send + 2 * chunk + group,
                self.recv + 2 * slot + group,
                device,
            )

        def sums(self, chunk):
            own, pair = turned(self.own_rows[chunk]), turned(self.pair_rows[chunk])

            def tile_sums(group, tile):
                at = slice(tile * self.depth, (tile + 1) * self.depth) if self.split else slice(None)
                column = 0 if self.split else tile
                part = contract(own[at], self.own_columns(group, column), 1, 0)
                return part + contract(pair[at], self.pair_columns(group, column), 1, 0)

            return tile_sums

        def add(self, rank, chunk, slot, device):
            tile_sums = self.sums(chunk)
            self.free(chunk, device)
            if self.ends is not None:

                @pl.when(rank == 1)
                def _():
                    self.bring_end(chunk)

            for group in range(2):
                half = self.half(group)

                @pl.when(rank > (0 if self.ends is None else 1))
                def _():
                    self.copy(chunk, group, chunk, device).wait_recv()
                    bring = local(self.land.at[chunk, half], self.got, self.local)
                    bring.start()
                    bring.wait()

                if self.ends is None:

                    @pl.when(rank == 0)
                    def _():
                        self.got[...] = jnp.zeros_like(self.got)

                else:

                    @pl.when(rank == 1)
                    def _():
                        self.end_sums(group)

                for tile in range(self.count):
                    whole = tile_sums(group, tile) + self.got[tile].astype(f32)
                    self.stage[chunk, half, tile] = whole.astype(bf16)
                self.copy(chunk, group, slot, device).start()

        def free(self, chunk, device):
            if self.earlier is not None:

                @pl.when(jnp.logical_not(at_end))
                def _():
                    for group in range(2):
                        self.earlier.copy(chunk, group, chunk, device).wait_send()

        def bring_end(self, chunk):
            self.ends.bring(chunk)
            copies = []
            for pair in range(2):
                rows_in = self.ends.land.at[chunk, pair]
                copies.append(local(rows_in, r["weight"].at[1, pair, :rows, : rows_in.shape[1]], stream_base + pair))
                for part in range(2):
                    at = r["weight"].at[0, pair, part * rows : (part + 1) * rows, :q]
                    copies.append(local(r["end_cot"].at[pair, part], at, stream_base + 2 + 2 * pair + part))
            for copy in copies:
                copy.start()
            for copy in copies:
                copy.wait()

        def end_sums(self, group):
            columns = self.depth * self.count if self.split else self.depth
            for tile in range(self.count):
                at = slice(tile * self.depth, (tile + 1) * self.depth)
                total = None
                for pair in range(2):
                    left = turned(r["weight"][1, pair, :rows, :columns][:, at])
                    part = contract(left, r["weight"][0, pair, group * rows : (group + 1) * rows, :q], 1, 0)
                    total = part if total is None else total + part
                self.got[tile] = total.astype(bf16)

        def start(self, tile):
            for way, end, device in ((0, 0, right), (1, line - 1, left)):

                @pl.when(place == end)
                def _():
                    chunk = (line - 1) * (1 - way)
                    if tile == 0:
                        self.free(chunk, device)
                    tile_sums = self.sums(chunk)
                    for group in range(2):
                        half = self.half(group)
                        self.stage[chunk, half, tile] = tile_sums(group, tile).astype(bf16)
                        remote(
                            self.stage.at[chunk, half, tile],
                            self.land.at[chunk, half, tile],
                            self.send + 2 * chunk + group,
                            self.recv + 2 * chunk + group,
                            device,
                        ).start()

        def step(self, number):
            def one(way, carry):
                rightward = way == 0
                rank = jnp.where(rightward, place, line - 1 - place)
                chunk = jnp.where(rightward, line - 1 - number + place, place - (line - 1) + number)
                slot = jnp.where(chunk == place + 1 - 2 * way, line + way, chunk)
                device = {"dp": dp + 2 - 4 * way}

                @pl.when((rank <= number) & (rank < line - 1) & (rank >= (0 if self.ends is None else 1)))
                def _():
                    self.add(rank, chunk, slot, device)

                return carry

            lax.fori_loop(0, 2, one, 0)

        def steps(self, first, last):
            if last - first == 1:
                self.step(first)
            elif last > first:
                loop(first, last, self.step)

        def own(self):
            if self.earlier is not None:
                self.earlier.out.wait()
                self.earlier.later = True
            tile_sums = self.sums(place)
            if self.ends is not None:

                @pl.when(near_end)
                def _():
                    self.bring_end(place)

            for group in range(2):
                if self.ends is not None:

                    @pl.when(near_end)
                    def _():
                        self.end_sums(group)

                    @pl.when(jnp.logical_not(near_end))
                    def _():
                        self.got[...] = jnp.zeros_like(self.got)

                for tile in range(self.count):
                    whole = tile_sums(group, tile)
                    if self.ends is not None:
                        whole = whole + self.got[tile].astype(f32)
                    self.stage[place, self.half(group), tile] = whole.astype(bf16)
            self.out = local(self.stage.at[place], r["own_" + self.name], self.local)
            self.out.start()

        def finish(self):
            if not self.later:
                self.out.wait()
            far = 0 if self.ends is None else 1
            for group in range(2):

                @pl.when(place > far)
                def _():
                    self.copy(place, group, line, left).wait_recv()

                @pl.when(place < line - 1 - far)
                def _():
                    self.copy(place, group, line + 1, right).wait_recv()

            def sent(chunk):
                @pl.when((chunk != place) & (jnp.logical_not(at_end) if far else True))
                def _():
                    for group in range(2):
                        self.copy(chunk, group, chunk, right).wait_send()

            if not self.later:
                loop(0, line, sent)

    cot_own_tile = lambda group, tile: r["cotq"][0, group]
    cot_pair_tile = lambda group, tile: r["cotp"][group]
    down = Flow("down", r["act_own"], r["act_pair"], cot_own_tile, cot_pair_tile, split=True, ends=end_act)
    up = Flow(
        "up",
        r["hid_own"],
        r["hid_pair"],
        lambda group, tile: r[("db_mine", "db_theirs")[group]][tile],
        lambda group, tile: r[("db_mine_pair", "db_theirs_pair")[group]][tile],
        by_col=True,
        earlier=down if shared else None,
    )
    dense = Flow("dense", r["att_own"], r["att_pair"], cot_own_tile, cot_pair_tile, ends=end_att)
    qkv = Flow(
        "qkv",
        r["hid_own"],
        r["hid_pair"],
        lambda group, tile: r[("dp_mine", "dp_theirs")[group]][tile],
        lambda group, tile: r[("dp_mine_pair", "dp_theirs_pair")[group]][tile],
        by_col=True,
    )
    cuts = (0, 1, line // 2, line - 1)

    swaps["qkv"].wait()

    def qkv_work(step, slot):
        part = contract(r["hid"][0], r["weight"][slot, 0, :, :PAIR_QKV], 1, 0)
        part = part + contract(r["hid"][1], r["weight"][slot, 1, :, :PAIR_QKV], 1, 0)
        r["total"][step, :, :PAIR_QKV] = part + r["qkv_b"][step]

    stream(pairs, column_tiles("qkv", PAIR_QKV), qkv_work)
    swaps["dense"].wait()

    def dense_work(step, slot):
        d_mixed = over_weight_rows(slot, z.features, lambda h, p: r["cotq"][h, p]).astype(bf16)
        for pair in range(pairs):
            r["mixed"][pair] = d_mixed[:, pair * PAIR : (pair + 1) * PAIR]

    stream(1, row_tiles("dense", z.features), dense_work)
    loop(0, 1, pass_on(act_side, act_on))
    loop(0, 1, waits(act_on))
    end_act.start(True, 0, 1)

    att_side_send, att_side_recv = take("send", half_line), take("recv", half_line)
    att_col_send, att_col_recv = take("send", half_line), take("recv", half_line)
    att_on_send, att_on_recv = take("send", half_line), take("recv", half_line)

    def att_side(k):
        slot = col * half_line + k
        return remote(
            r["att_part"].at[2 * k + other_side], r["att_pair"].at[slot], att_side_send + k, att_side_recv + k, to_side
        )

    def att_col(k):
        slot = col * half_line + k
        return remote(r["att_own"].at[slot], r["att_own"].at[slot], att_col_send + k, att_col_recv + k, to_col)

    def att_on(k):
        slot = col * half_line + k
        return remote(r["att_pair"].at[slot], r["att_pair"].at[slot], att_on_send + k, att_on_recv + k, to_col)

    def head_pair(pair):
        attended, d_projected = attention_pair(
            r["total"][pair, :, :PAIR_QKV], r["mixed"][pair], r["tables"], r["seg_col"][...], r["seg_row"][...]
        )
        r["dp_mine"][pair] = d_projected
        dp_side(pair).start()
        dp_col(pair).start()
        sums = jnp.sum(d_projected.astype(f32), axis=0, keepdims=True)
        r["sums"][:, pl.ds(pl.multiple_of(2 * q + pair * PAIR_QKV, 128), PAIR_QKV)] = sums
        r["att"][:, pl.ds(pl.multiple_of(pair * PAIR, PAIR), PAIR)] = attended
        each = PAIR // z.dense_chunk
        for part in range(each):
            chunk = pair * each + part
            k = chunk // 2
            piece = attended[:, part * z.dense_chunk : (part + 1) * z.dense_chunk]

            @pl.when(lax.rem(chunk, 2) == side)
            def _():
                r["att_own"][col * half_line + k] = piece
                att_col(k).start()

            @pl.when(lax.rem(chunk, 2) == other_side)
            def _():
                r["att_part"][chunk] = piece
                att_side(k).start()

    loop(0, pairs // 2, head_pair)
    cot_side_onward.wait()
    send_end_cot(1, other_row)
    loop(1, half_line, pass_on(act_side, act_on))
    loop(1, half_line, waits(act_on))
    end_act.start(True, 1, line - 1)
    loop(pairs // 2, pairs, head_pair)

    def near_end_cot():
        @pl.when(near_end)
        def _():
            for pair in range(2):
                for part in range(2):
                    end_cot(pair, part, outward).wait_recv()

    near_end_cot()
    down.steps(cuts[1], cuts[2])

    def scatter(name, total, earlier=None):
        across = Message(r["part_send"], r[name + "_got"], to_col)
        over = Message(r["part_row"], r[name + "_row"], to_row)

        def free(message):
            message.copy().wait_send()
            pending.remove(message)

        def first():
            if earlier is not None:
                free(earlier[0])
            for p in range(2):
                r["part_send"][p] = total[2 + p].astype(bf16)
            across.start()

        def second():
            across.wait()
            if earlier is not None:
                free(earlier[1])
            for p in range(2):
                total[p] = total[p] + r[name + "_got"][p].astype(f32)
            r["part_row"][...] = total[other_row].astype(bf16)
            over.start()

        def third():
            over.wait()
            return total[row] + r[name + "_row"][...].astype(f32)

        return first, second, third, (across, over)

    total = r["total"]

    def down_out(step, slot):
        for h in range(2):
            for p in range(2):
                part = contract(r["act"][step], r["weight"][slot, h, p * q : p * q + z.down_chunk, :], 1, 0)

                @pl.when(step == 0)
                def _():
                    total[2 * h + p] = part

                @pl.when(step > 0)
                def _():
                    total[2 * h + p] = total[2 * h + p] + part

    def dense_out(step, slot):
        for h in range(2):
            for p in range(2):
                part = contract(r["att"][...], r["weight"][slot, h, p * q : p * q + z.features, :], 1, 0)
                total[2 * h + p] = total[2 * h + p] + part

    def up_back(step, slot):
        for h in range(2):
            for p in range(2):
                part = contract(r["db_mine"][step], r["weight"][slot, h, p * q : (p + 1) * q, : z.down_chunk], 1, 1)

                @pl.when(step == 0)
                def _():
                    total[2 * h + p] = part

                @pl.when(step > 0)
                def _():
                    total[2 * h + p] = total[2 * h + p] + part

    def qkv_back(step, slot):
        for h in range(2):
            for p in range(2):
                part = contract(r["dp_mine"][step], r["weight"][slot, h, p * q : (p + 1) * q, :PAIR_QKV], 1, 1)
                total[2 * h + p] = total[2 * h + p] + part

    stream(tiles, column_tiles("up", z.down_chunk), up_back)
    stream(pairs, column_tiles("qkv", PAIR_QKV), qkv_back)
    dh_first, dh_second, dh_third, dh_messages = scatter("dh", total)
    dh_first()
    hid_side.wait()
    for tile in range(tiles):
        loop(tile, tile + 1, pass_on(db_side, db_on))
        loop(tile, tile + 1, waits(db_col, db_on))
        up.start(tile)
        if tile == tiles // 2:
            down.steps(cuts[2], cuts[3])
    dh_second()
    up.steps(cuts[1], cuts[2])

    d_hidden = dh_third()
    r["grad_inputs"][...] = d_hidden
    own_in = r["inq"].at[0, row]
    gain = r["gainq"][0, row, 0:1, :]
    sums_row = Message(r["sum_send"].at[0], r["sum_got"].at[0], to_row)
    sums_col = Message(r["sum_send"].at[1], r["sum_got"].at[1], to_col)
    normed = (own_in[...].astype(f32) - r["stat"][0]) * r["stat"][1]
    d_normed = d_hidden * gain
    lane = lax.broadcasted_iota(jnp.int32, (rows, 128), 1)
    one = jnp.sum(d_normed, axis=1, keepdims=True)
    two = jnp.sum(d_normed * normed, axis=1, keepdims=True)
    packed = jnp.where(lane == 0, one, jnp.where(lane == 1, two, 0.0))
    r["sum_send"][0] = turned(packed)[:8]
    sums_row.start()
    r["sums"][:, 0:q] = jnp.sum(d_hidden * normed, axis=0, keepdims=True)
    r["sums"][:, q : 2 * q] = jnp.sum(d_hidden, axis=0, keepdims=True)
    r["sums"][:, 2 * q + z.qkv + z.hidden :] = jnp.sum(r["cotq"][0, row].astype(f32), axis=0, keepdims=True)
    small_side = Message(r["sums"], r["sums_got"].at[0], to_side)
    small_side.start()

    stream(tiles, row_tiles("down", z.down_chunk), down_out)
    stream(1, row_tiles("dense", z.features), dense_out)
    out_first, out_second, out_third, out_messages = scatter("out", total, dh_messages)
    out_first()
    sums_row.wait()
    r["sum_send"][1] = r["sum_send"][0] + r["sum_got"][0]
    sums_col.start()
    up.steps(cuts[2], cuts[3])
    out_second()
    sums_col.wait()
    both = r["sum_send"][1] + r["sum_got"][1]
    spread = turned(jnp.concatenate([both, jnp.zeros((120, rows), f32)], axis=0))
    part_one, part_two = spread[:, 0:1] / z.width, spread[:, 1:2] / z.width
    normed = (own_in[...].astype(f32) - r["stat"][0]) * r["stat"][1]
    d_normed = r["grad_inputs"][...] * gain
    r["grad_inputs"][...] = cot[...].astype(f32) + r["stat"][1] * (d_normed - part_one - normed * part_two)

    small_send, small_recv = take("send", 2), take("recv", 2)

    def small(way, device):
        return remote(r["sums_send"].at[way], r["sums_got"].at[1 + way], small_send + way, small_recv + way, device)

    def hop(number):
        for way, rank, device, last in ((0, place, right, has_right), (1, line - 1 - place, left, has_left)):

            @pl.when((rank == number) & last)
            def _():
                @pl.when(rank == 0)
                def _():
                    r["sums_send"][way] = r["sums"][...]

                @pl.when(rank > 0)
                def _():
                    small(way, device).wait_recv()
                    r["sums_send"][way] = r["sums"][...] + r["sums_got"][1 + way]

                small(way, device).start()

    def hops(first, last):
        if last - first == 1:
            hop(first)
        elif last > first:
            loop(first, last, hop)

    loop(0, pairs, pass_on(dp_side, dp_on))
    loop(0, half_line, pass_on(att_side, att_on))
    loop(0, half_line, waits(att_col, att_on))
    end_att.start(False, 0, line - 1)
    end_att.start(True, 0, line - 1)
    loop(0, pairs, waits(dp_col, dp_on))
    qkv.steps(cuts[0], cuts[1])
    branch = out_third()
    bias = as_row(r["out_bias"][...])
    valid = (r["seg_col"][...] < z.seqs).astype(f32)
    r["outputs"][...] = (r["inq"][0, row].astype(f32) + valid * (branch + bias)).astype(bf16)
    small_side.wait()
    small_side.copy().wait_send()
    pending.remove(small_side)
    r["sums"][...] = r["sums"][...] + r["sums_got"][0]
    hops(cuts[0], cuts[1])
    down.own()
    dense.steps(cuts[1], cuts[2])
    qkv.steps(cuts[1], cuts[2])
    hops(cuts[1], cuts[2])
    up.own()
    dense.steps(cuts[2], cuts[3])
    qkv.steps(cuts[2], cuts[3])
    hops(cuts[2], cuts[3])
    dense.own()
    qkv.own()

    r["small"][...] = r["sums"][...]

    @pl.when(place == line - 1)
    def _():
        small(0, left).wait_recv()

    @pl.when(place == 0)
    def _():
        small(1, right).wait_recv()

    @pl.when(has_left)
    def _():
        r["small"][...] = r["small"][...] + r["sums_got"][1]

    @pl.when(has_right)
    def _():
        r["small"][...] = r["small"][...] + r["sums_got"][2]

    @pl.when(has_right)
    def _():
        small(0, right).wait_send()

    @pl.when(has_left)
    def _():
        small(1, left).wait_send()

    for flow in (down, up, dense, qkv):
        flow.finish()
    end_act.finish()
    end_att.finish()

    @pl.when(at_end)
    def _():
        for pair in range(2):
            for part in range(2):
                end_cot(pair, part, inward).wait_send()

    for message in pending:
        message.copy().wait_send()

    def sent(*copies):
        def work(k):
            for copy in copies:
                copy(k).wait_send()

        return work

    loop(0, half_line, sent(act_side, act_col, act_on, att_side, att_col, att_on))
    loop(0, tiles, sent(db_side, db_col, db_on))
    loop(0, pairs, sent(dp_side, dp_col, dp_on))
    assert marks["send"] <= SENDS * line and marks["recv"] <= SENDS * line and marks["local"] <= 16


def on_device(
    dp_size,
    inputs,
    norm_gain,
    norm_shift,
    qkv_weight,
    qkv_bias,
    up_weight,
    up_bias,
    dense_weight,
    down_weight,
    out_bias,
    cotangent,
    seq_lengths,
    seq_owner,
):
    z = Sizes(dp_size, inputs, qkv_weight, up_weight, dense_weight, down_weight, seq_lengths)
    if not fits(z):
        return on_device_plain(
            dp_size,
            inputs,
            norm_gain,
            norm_shift,
            qkv_weight,
            qkv_bias,
            up_weight,
            up_bias,
            dense_weight,
            down_weight,
            out_bias,
            cotangent,
            seq_lengths,
            seq_owner,
        )
    rows, q, line = z.rows, z.quarter, z.line
    lane_rate = np.zeros((1, HEAD_DIM), np.float32)
    lane_rate[0, :ROT] = rope_base ** (-2.0 * (np.arange(ROT) % HALF_ROT) / ROT)
    operands = dict(
        inputs=(inputs, pl.ANY),
        cot=(cotangent, pltpu.VMEM),
        norm_gain=(norm_gain, pltpu.VMEM),
        norm_shift=(norm_shift, pltpu.VMEM),
        qkv_bias=(qkv_bias, pltpu.VMEM),
        up_bias=(up_bias, pltpu.VMEM),
        out_bias=(out_bias, pltpu.VMEM),
        frequency=(jnp.asarray(lane_rate), pltpu.VMEM),
        seq_lengths=(seq_lengths, pltpu.SMEM),
        seq_owner=(seq_owner, pltpu.SMEM),
        up_w=(up_weight, pl.ANY),
        down_w=(down_weight, pl.ANY),
        qkv_w=(qkv_weight, pl.ANY),
        dense_w=(dense_weight, pl.ANY),
    )
    results = dict(
        outputs=((rows, q), bf16, pltpu.VMEM),
        grad_inputs=((rows, q), f32, pltpu.VMEM),
        small=((1, 3 * q + z.qkv + z.hidden), f32, pltpu.VMEM),
        up_o=((z.half, z.hidden), bf16, pl.ANY),
        down_o=((z.hidden, z.half), bf16, pl.ANY),
        qkv_o=((z.half, z.qkv), bf16, pl.ANY),
        dense_o=((z.features, z.half), bf16, pl.ANY),
        end_cot=((2, 2, rows, q), bf16, pl.ANY),
        end_act=((line, 2, rows, z.down_chunk), bf16, pl.ANY),
        end_att=((line, 2, rows, z.dense_chunk), bf16, pl.ANY),
    )
    for name, shape in flows_of(z).items():
        results["land_" + name] = ((line + 2, 2) + shape, bf16, pl.ANY)
        results["own_" + name] = ((2,) + shape, bf16, pl.ANY)
    scratch = scratch_of(z)
    names = list(operands) + list(results) + list(scratch) + ["send_sem", "recv_sem", "local_sem"]
    found = pl.pallas_call(
        partial(layer_kernel, z, names),
        in_specs=[pl.BlockSpec(memory_space=space) for value, space in operands.values()],
        out_specs=[pl.BlockSpec(memory_space=space) for shape, kind, space in results.values()],
        out_shape=[jax.ShapeDtypeStruct(shape, kind) for shape, kind, space in results.values()],
        scratch_shapes=[pltpu.VMEM(shape, kind) for shape, kind in scratch.values()]
        + [pltpu.SemaphoreType.DMA((SENDS * line,)), pltpu.SemaphoreType.DMA((SENDS * line,)), pltpu.SemaphoreType.DMA((16,))],
        compiler_params=pltpu.CompilerParams(
            collective_id=0, has_side_effects=True, vmem_limit_bytes=VMEM_LIMIT
        ),
        name="layer",
    )(*[value for value, space in operands.values()])
    got = dict(zip(results, found))
    big, small = finish(z, got)
    return (
        big["outputs"],
        big["grad_inputs"],
        small["gain"],
        small["shift"],
        big["qkv"],
        small["qkv"],
        big["up"],
        small["up"],
        big["dense"],
        big["down"],
        small["out"],
    )


def finish(z, got):
    line, steps = z.line, 8
    flows = flows_of(z)
    names = list(flows)
    pieces = dict(gain=z.quarter, shift=z.quarter, qkv=z.qkv, up=z.hidden, out=z.quarter)

    def kernel(*refs):
        place = lax.axis_index("dp") // 2
        fed = refs[: 3 * len(names) + 3]
        made = refs[3 * len(names) + 3 :]
        for index in range(len(names)):
            own, from_left, from_right = (ref[...].astype(f32) for ref in fed[3 * index : 3 * index + 3])
            far = 1 if names[index] in ("down", "dense") else 0
            total = own + jnp.where(place > far, from_left, 0.0) + jnp.where(place < line - 1 - far, from_right, 0.0)
            made[index][...] = total.reshape(made[index].shape)
        outputs, grad_inputs, small = fed[3 * len(names) :]
        made[len(names)][...] = outputs[...]
        made[len(names) + 1][...] = grad_inputs[...]

        @pl.when(pl.program_id(0) == 0)
        def _():
            start = 0
            for index, width in enumerate(pieces.values()):
                made[len(names) + 2 + index][...] = small[:, start : start + width].reshape(width)
                start += width

    in_specs, out_specs, out_shape, fed = [], [], [], []
    for name in names:
        count, depth, each = flows[name]
        group = count // (steps // 2) or 1

        def tile_index(step, name=name):
            half, tile = step // (steps // 2), lax.rem(step, steps // 2)
            return half, tile if flows[name][0] >= steps // 2 else 0

        block = (None, group, depth, each)
        land_block = (None, None, group, depth, each)
        in_specs.append(pl.BlockSpec(block, lambda i, f=tile_index: (*f(i), 0, 0)))
        in_specs.append(pl.BlockSpec(land_block, lambda i, f=tile_index: (line, *f(i), 0, 0)))
        in_specs.append(pl.BlockSpec(land_block, lambda i, f=tile_index: (line + 1, *f(i), 0, 0)))
        fed += [got["own_" + name], got["land_" + name], got["land_" + name]]
        if name == "down":
            out_shape.append(jax.ShapeDtypeStruct((count * depth, 2 * each), f32))
            out_specs.append(pl.BlockSpec((group * depth, each), lambda i, f=tile_index: f(i)[::-1]))
        else:
            assert group == 1
            out_shape.append(jax.ShapeDtypeStruct((depth, 2 * count * each), f32))
            out_specs.append(
                pl.BlockSpec((depth, each), lambda i, f=tile_index, count=count: (0, f(i)[0] * count + f(i)[1]))
            )
    for name in ("outputs", "grad_inputs"):
        rows, columns = got[name].shape
        spec = pl.BlockSpec((rows // steps, columns), lambda i: (i, 0))
        in_specs.append(spec)
        out_specs.append(spec)
        out_shape.append(jax.ShapeDtypeStruct((rows, columns), got[name].dtype))
        fed.append(got[name])
    in_specs.append(pl.BlockSpec(memory_space=pltpu.VMEM))
    fed.append(got["small"])
    for width in pieces.values():
        out_specs.append(pl.BlockSpec(memory_space=pltpu.VMEM))
        out_shape.append(jax.ShapeDtypeStruct((width,), f32))
    made = pl.pallas_call(
        kernel, grid=(steps,), in_specs=in_specs, out_specs=out_specs, out_shape=out_shape, name="finish"
    )(*fed)
    big = dict(zip(names + ["outputs", "grad_inputs"], made))
    return big, dict(zip(pieces, made[len(names) + 2 :]))


def attention_kernel(proj_ref, mixed_ref, tables_ref, seg_col_ref, seg_row_ref, attended_ref, grad_ref):
    attended_ref[...], grad_ref[...] = attention_pair(
        proj_ref[...], mixed_ref[...], tables_ref, seg_col_ref[...], seg_row_ref[...]
    )


def attention(projected, mixed, tables, segment):
    rows, width = projected.shape
    pairs = width // PAIR_QKV
    return pl.pallas_call(
        attention_kernel,
        grid=(pairs,),
        in_specs=[
            pl.BlockSpec((rows, PAIR_QKV), lambda i: (0, i)),
            pl.BlockSpec((rows, PAIR), lambda i: (0, i)),
            pl.BlockSpec((3, rows, HEAD_DIM), lambda i: (0, 0, 0)),
            pl.BlockSpec((rows, 1), lambda i: (0, 0)),
            pl.BlockSpec((1, rows), lambda i: (0, 0)),
        ],
        out_specs=[
            pl.BlockSpec((rows, PAIR), lambda i: (0, i)),
            pl.BlockSpec((rows, PAIR_QKV), lambda i: (0, i)),
        ],
        out_shape=[
            jax.ShapeDtypeStruct((rows, pairs * PAIR), bf16),
            jax.ShapeDtypeStruct((rows, width), bf16),
        ],
        compiler_params=pltpu.CompilerParams(vmem_limit_bytes=48 * 1024 * 1024),
        cost_estimate=pl.CostEstimate(
            flops=14 * 2 * pairs * rows * rows * HEAD_DIM * 2,
            bytes_accessed=rows * width * 7,
            transcendentals=2 * pairs * rows * rows,
        ),
        name="attention",
    )(projected, mixed, tables, segment[:, None], segment[None, :])


def dot_plain(left, right):
    return jnp.dot(left, right, preferred_element_type=f32)


def contract_rows(left, right):
    return lax.dot_general(left, right, (((0,), (0,)), ((), ())), preferred_element_type=f32)


def contract_cols(left, right):
    return lax.dot_general(left, right, (((1,), (1,)), ((), ())), preferred_element_type=f32)


def on_device_plain(
    dp_size,
    inputs,
    norm_gain,
    norm_shift,
    qkv_weight,
    qkv_bias,
    up_weight,
    up_bias,
    dense_weight,
    down_weight,
    out_bias,
    cotangent,
    seq_lengths,
    seq_owner,
):
    row_count = inputs.shape[0]
    line = dp_size // 2
    device = lax.axis_index("dp")
    place = device // 2
    side = device % 2
    row = lax.axis_index("row")
    col = lax.axis_index("col")

    over_row = partial(lax.ppermute, axis_name="row", perm=[(0, 1), (1, 0)])
    over_col = partial(lax.ppermute, axis_name="col", perm=[(0, 1), (1, 0)])
    over_side = partial(lax.ppermute, axis_name="dp", perm=[(e, e ^ 1) for e in range(dp_size)])

    def in_order(index, mine, other, axis):
        first = jnp.where(index == 0, mine, other)
        second = jnp.where(index == 0, other, mine)
        return jnp.concatenate([first, second], axis=axis)

    def half_at(array, index, axis):
        width = array.shape[axis] // 2
        return lax.dynamic_slice_in_dim(array, index * width, width, axis)

    segment, position, is_valid = layout(seq_lengths, seq_owner, device, row_count)
    tables = rotation_tables(position)

    gains = jnp.stack([norm_gain, norm_shift])
    grad_branch = cotangent * is_valid.astype(bf16)[:, None]
    inputs_half = in_order(row, inputs, over_row(inputs), 1)
    gains_half = in_order(row, gains, over_row(gains), 1)
    inputs_other = over_col(inputs_half)
    gains_other = over_col(gains_half)
    branch_half = in_order(row, grad_branch, over_row(grad_branch), 1)
    branch_other = over_col(branch_half)

    up_mine, up_other = half_at(up_weight, col, 1), over_col(half_at(up_weight, 1 - col, 1))
    down_mine, down_other = half_at(down_weight, col, 0), over_col(half_at(down_weight, 1 - col, 0))
    qkv_mine, qkv_other = half_at(qkv_weight, col, 1), over_col(half_at(qkv_weight, 1 - col, 1))
    dense_mine, dense_other = half_at(dense_weight, col, 0), over_col(half_at(dense_weight, 1 - col, 0))

    width = 4 * inputs.shape[1]
    source, source_other = inputs_half.astype(f32), inputs_other.astype(f32)
    average = (jnp.sum(source, axis=1) + jnp.sum(source_other, axis=1)) / width
    square = (jnp.sum(source * source, axis=1) + jnp.sum(source_other * source_other, axis=1)) / width
    scale_inv = lax.rsqrt(square - average * average + epsilon)[:, None]

    def hidden_of(rows_in, gain_pair):
        normed = (rows_in - average[:, None]) * scale_inv
        pair = gain_pair.astype(f32)
        return (normed * pair[0] + pair[1]).astype(bf16)

    hidden, hidden_other = hidden_of(source, gains_half), hidden_of(source_other, gains_other)

    before = dot_plain(hidden, up_mine) + dot_plain(hidden_other, up_other) + up_bias.astype(f32)
    activated = jax.nn.gelu(before, approximate=True).astype(bf16)
    d_activated = contract_cols(branch_half, down_mine) + contract_cols(branch_other, down_other)
    unused_value, gelu_back = jax.vjp(partial(jax.nn.gelu, approximate=True), before)
    d_before = gelu_back(d_activated)[0].astype(bf16)

    projected = dot_plain(hidden, qkv_mine) + dot_plain(hidden_other, qkv_other) + qkv_bias.astype(f32)
    d_mixed = (contract_cols(branch_half, dense_mine) + contract_cols(branch_other, dense_other)).astype(bf16)
    attended, d_projected = attention(projected, d_mixed, tables, segment)

    def chunks_of(array, index):
        rows, columns = array.shape
        grouped = array.reshape(rows, columns // (2 * chunk), 2, chunk)
        return lax.dynamic_index_in_dim(grouped, index, 2, keepdims=False).reshape(rows, columns // 2)

    branch_pair = over_side(branch_half)

    def feature_sums(array):
        kept = chunks_of(array, side)
        got = over_side(chunks_of(array, 1 - side))
        own = in_order(col, kept, over_col(kept), 1)
        pair = in_order(col, got, over_col(got), 1)
        return (contract_rows(own, branch_half) + contract_rows(pair, branch_pair)).astype(bf16)

    def along_line(sums):
        depth = sums.shape[0] // line
        parts = sums.reshape(line, depth, sums.shape[1])

        def part(index):
            return lax.dynamic_index_in_dim(parts, jnp.clip(index, 0, line - 1), 0, keepdims=False).astype(f32)

        rightward, leftward = None, None
        for step in range(line - 1):
            right_part = part(line - 1 - step + place)
            left_part = part(place - (line - 1) + step)
            if step:
                right_part = right_part + rightward.astype(f32)
                left_part = left_part + leftward.astype(f32)
            to_right = [(2 * z + x, 2 * z + 2 + x) for z in range(min(step + 1, line - 1)) for x in range(2)]
            to_left = [(dp_size - 1 - p, dp_size - 1 - q) for p, q in to_right]
            rightward = lax.ppermute(right_part.astype(bf16), "dp", to_right)
            leftward = lax.ppermute(left_part.astype(bf16), "dp", to_left)
        return part(place) + rightward.astype(f32) + leftward.astype(f32)

    chunk = down_weight.shape[0] // dp_size
    grad_down = along_line(feature_sums(activated))

    chunk = up_weight.shape[0] // dp_size
    hidden_own = chunks_of(hidden, side)
    hidden_pair = over_side(chunks_of(hidden, 1 - side))

    def hidden_sums(array):
        pair = over_side(array)
        mine = (contract_rows(hidden_own, array) + contract_rows(hidden_pair, pair)).astype(bf16)
        theirs = (contract_rows(hidden_own, over_col(array)) + contract_rows(hidden_pair, over_col(pair))).astype(bf16)
        return in_order(col, along_line(mine), along_line(theirs), 1)

    grad_up = hidden_sums(d_before)
    chunk = dense_weight.shape[0] // dp_size
    grad_dense = along_line(feature_sums(attended))
    grad_qkv = hidden_sums(d_projected)

    def scatter(mine, other):
        half = mine + over_col(other.astype(bf16)).astype(f32)
        return half_at(half, row, 1) + over_row(half_at(half, 1 - row, 1).astype(bf16)).astype(f32)

    branch = scatter(
        dot_plain(attended, dense_mine) + dot_plain(activated, down_mine),
        dot_plain(attended, dense_other) + dot_plain(activated, down_other),
    )
    valid_col = is_valid.astype(f32)[:, None]
    outputs = (inputs.astype(f32) + valid_col * (branch + out_bias.astype(f32))).astype(bf16)

    d_hidden = scatter(
        contract_cols(d_projected, qkv_mine) + contract_cols(d_before, up_mine),
        contract_cols(d_projected, qkv_other) + contract_cols(d_before, up_other),
    )
    normed = (inputs.astype(f32) - average[:, None]) * scale_inv
    d_normed = d_hidden * norm_gain.astype(f32)
    row_sums = jnp.stack([jnp.sum(d_normed, axis=1), jnp.sum(d_normed * normed, axis=1)])
    row_sums = row_sums + over_row(row_sums)
    row_sums = row_sums + over_col(row_sums)
    grad_inputs = cotangent.astype(f32) + scale_inv * (
        d_normed - row_sums[0][:, None] / width - normed * row_sums[1][:, None] / width
    )

    small = [
        jnp.sum(d_hidden * normed, axis=0),
        jnp.sum(d_hidden, axis=0),
        jnp.sum(d_projected.astype(f32), axis=0),
        jnp.sum(d_before.astype(f32), axis=0),
        jnp.sum(grad_branch.astype(f32), axis=0),
    ]
    together = jnp.concatenate(small)
    bit = 1
    while bit < dp_size:
        together = together + lax.ppermute(together, "dp", [(e, e ^ bit) for e in range(dp_size)])
        bit *= 2
    ends = []
    for piece in small:
        ends.append((ends[-1] if ends else 0) + piece.shape[0])
    grad_gain, grad_shift, grad_qkv_bias, grad_up_bias, grad_out_bias = jnp.split(together, ends[:-1])
    return (
        outputs,
        grad_inputs,
        grad_gain,
        grad_shift,
        grad_qkv,
        grad_qkv_bias,
        grad_up,
        grad_up_bias,
        grad_dense,
        grad_down,
        grad_out_bias,
    )


def solution(mesh):
    in_specs = (
        P("dp", ("col", "row")),
        P(("col", "row")),
        P(("col", "row")),
        P("col", "row"),
        P(("row", "col")),
        P("col", "row"),
        P(("row", "col")),
        P("row", "col"),
        P("row", "col"),
        P(("col", "row")),
        P("dp", ("col", "row")),
        P(),
        P(),
    )
    out_specs = (
        P("dp", ("col", "row")),
        P("dp", ("col", "row")),
        P(("col", "row")),
        P(("col", "row")),
        P(("col", "dp"), "row"),
        P(("row", "col")),
        P(("col", "dp"), "row"),
        P(("row", "col")),
        P(("row", "dp"), "col"),
        P(("row", "dp"), "col"),
        P(("col", "row")),
    )
    return jax.shard_map(
        partial(on_device, mesh.shape["dp"]), mesh=mesh, in_specs=in_specs, out_specs=out_specs, check_vma=False
    )
```

profile of v0, /device:TPU:9, one launch (start us, length us, event | category | flops | bytes accessed | tf_op | source)
XLA Modules:
  0.0 260.6 jit_solution(13974768502749521088)
XLA Ops:
  0.6 249.4 %layer.1 = (bf16[512,512]{1,0:T(8,128)(2,1)}, f32[512,512]{1,0:T(8,128)}, f32[1,5120]{1,0:T(1,128)}, bf16[1024,2048]{1,0:T(8,128)(2,1)}, bf16[2048,1024]{1,0:T(8...) custom-call(bf16[512,512]{1,0:T(8,128)(2,1)} %refs_0_.1, ...), custom_call_target="tpu_custom_call" | custom-call | tf_op jit(solution)/shard_map/layer/pallas_call | solution.py:1244
  250.1 10.2 %finish.1 = (f32[512,1024]{1,0:T(8,128)}, f32[128,4096]{1,0:T(8,128)}, f32[128,1024]{1,0:T(8,128)}, f32[128,3072]{1,0:T(8,128)}, bf16[512,512]{1,0:T(8,128)(2,1)...) custom-call(bf16[2,4,128,512]{3,2,1,0:T(8,128)(2,1)} %get-tuple-elem, ...), custom_call_target="tpu_custom_call" | custom-call | tf_op jit(solution)/shard_map/finish/pallas_call | solution.py:1335
where the time goes:
time: 265 us; the launch traced here: 261 us
  Pallas kernels  260 us (98%)
    pallas_call x1, Pallas kernels, on_device(): pl.pallas_call(partial(layer_kernel, z, names), in_specs=[pl.BlockSpec(me...  249 us
    pallas_call x1, Pallas kernels, finish(): pl.pallas_call(kernel, grid=(steps,), in_specs=in_specs, out_specs=out_sp...  10.2 us

commit v1 on v0

--- a/solution.py
+++ b/solution.py
@@ -21,6 +21,7 @@
 VMEM_LIMIT = 67_000_000
 SCRATCH_LIMIT = 58 * 1024 * 1024
 SENDS = 48
+LOCALS = 20
 score_scale = HEAD_DIM ** (-0.5)
 bf16 = jnp.bfloat16
 f32 = jnp.float32
@@ -171,9 +172,9 @@
         sums_got=((3, 1, 3 * q + z.qkv + z.hidden), f32),
         sums_send=((2, 1, 3 * q + z.qkv + z.hidden), f32),
         hid=((2, rows, z.half), bf16),
-        hid_own=((line, rows, up), bf16),
-        hid_send=((line, rows, up), bf16),
-        hid_pair=((line, rows, up), bf16),
+        hid_own=((rows, line * up), bf16),
+        hid_send=((rows, line * up), bf16),
+        hid_pair=((rows, line * up), bf16),
         stat=((2, rows, 1), f32),
         before=((tiles, rows, down), f32),
         act=((tiles, rows, down), bf16),
@@ -196,11 +197,8 @@
         st_down=((line, 2) + flows_of(z)["down"], bf16),
         st_up=((line, 2) + flows_of(z)["up"], bf16),
         st_dense=((line, 2) + flows_of(z)["dense"], bf16),
-        st_qkv=((line, 2) + flows_of(z)["qkv"], bf16),
         got_down=(flows_of(z)["down"], bf16),
-        got_up=(flows_of(z)["up"], bf16),
         got_dense=(flows_of(z)["dense"], bf16),
-        got_qkv=(flows_of(z)["qkv"], bf16),
         part_send=((2, rows, q), bf16),
         part_row=((rows, q), bf16),
         out_row=((rows, q), bf16),
@@ -208,10 +206,6 @@
         sum_send=((2, 8, rows), f32),
         sum_got=((2, 8, rows), f32),
     )
-    if shapes["before"][0] != (4, rows, q):
-        shapes["total"] = ((4, rows, q), f32)
-    if shapes["st_up"] == shapes["st_down"]:
-        del shapes["st_up"], shapes["got_up"]
     return shapes
 
 
@@ -219,19 +213,20 @@
     total = 0
     for shape, kind in scratch_of(z).values():
         total += math.prod(shape[:-1]) * -(-shape[-1] // 128) * 128 * jnp.dtype(kind).itemsize
-    return z.line >= 4 and z.line % 2 == 0 and total <= SCRATCH_LIMIT
+    flows = flows_of(z)
+    alike = flows["down"] == flows["up"] and flows["qkv"][:2] == flows["up"][:2] and flows["qkv"][2] <= flows["up"][2]
+    square = z.rows == z.quarter and (z.tiles, z.rows, z.down_chunk) == (4, z.rows, z.quarter)
+    return z.line == 4 and alike and square and total <= SCRATCH_LIMIT
 
 
 def layer_kernel(z, names, *refs):
     r = dict(zip(names, refs))
     rows, q, line, tiles, pairs = z.rows, z.quarter, z.line, z.tiles, z.pairs
     half_line = line // 2
-    if "total" not in r:
-        r["total"] = r["before"]
+    r["total"] = r["before"]
     r["dh_got"], r["out_got"] = r["inq"].at[1], r["cotq"].at[1]
-    shared = "st_up" not in r
-    if shared:
-        r["st_up"], r["got_up"] = r["st_down"], r["got_down"]
+    r["got_up"] = r["got_qkv"] = r["got_down"]
+    r["st_qkv"] = r["st_down"]
     dp = lax.axis_index("dp")
     row = lax.axis_index("row")
     col = lax.axis_index("col")
@@ -278,6 +273,12 @@
     has_right, has_left = place < line - 1, place > 0
     at_end, near_end = (place == 0) | (place == line - 1), (place == 1) | (place == line - 2)
     inward, outward = {"dp": dp + 2 - 4 * (place > 0)}, {"dp": dp + 2 - 4 * (place == 1)}
+    mate = {"dp": dp - 2 + 4 * (place == 1)}
+    first_half = place < line // 2
+
+    def counted(chunk):
+        return jnp.where(first_half, chunk, line - 1 - chunk)
+
     barrier = pltpu.get_barrier_semaphore()
     for device in (to_row, to_col, to_side):
         pl.semaphore_signal(barrier, inc=1, device_id=device, device_id_type=MESH)
@@ -391,10 +392,13 @@
 
                 loop(first, last, one)
 
-        def bring(self, chunk):
-            self.copy(chunk, outward, False).wait_recv()
-            self.onward(chunk).start()
-            self.onward(chunk).wait_recv()
+        def hand_over(self, *numbers):
+            @pl.when(near_end)
+            def _():
+                for number in numbers:
+                    chunk = counted(line - 1 - number)
+                    self.copy(chunk, outward, False).wait_recv()
+                    self.onward(chunk).start()
 
         def finish(self):
             def one(chunk):
@@ -485,8 +489,9 @@
     for c in range(line):
         even = r["hid"][0, :, 2 * c * z.up_chunk : (2 * c + 1) * z.up_chunk]
         odd = r["hid"][0, :, (2 * c + 1) * z.up_chunk : (2 * c + 2) * z.up_chunk]
-        r["hid_own"][c] = jnp.where(side == 0, even, odd)
-        r["hid_send"][c] = jnp.where(side == 0, odd, even)
+        at = slice(c * z.up_chunk, (c + 1) * z.up_chunk)
+        r["hid_own"][:, at] = jnp.where(side == 0, even, odd)
+        r["hid_send"][:, at] = jnp.where(side == 0, odd, even)
 
     def stream(count, copies, work):
         for copy in copies(jnp.int32(0), jnp.int32(0)):
@@ -570,9 +575,9 @@
         activated = gelu(before).astype(bf16)
         r["act"][tile] = activated
 
-        @pl.when(step < half_line)
+        @pl.when(step == 0)
         def _():
-            act_side(step).start()
+            act_side(0).start()
 
         @pl.when(step >= half_line)
         def _():
@@ -589,6 +594,11 @@
     cot_onward.start()
     cot_side_onward.start()
     send_end_cot(0, other_row)
+
+    def start_side(j):
+        act_side(j).start()
+
+    loop(1, half_line, start_side)
     loop(0, half_line, waits(act_col))
     end_act.start(False, 0, line - 1)
     swaps["qkv"].start()
@@ -639,228 +649,184 @@
     stream(tiles, row_tiles("down", z.down_chunk), down_work)
 
     class Flow:
-        def __init__(self, name, own_rows, pair_rows, own_columns, pair_columns, split=False, by_col=False, earlier=None, ends=None):
-            self.name, self.split, self.by_col, self.earlier, self.ends = name, split, by_col, earlier, ends
-            self.own_rows, self.pair_rows = own_rows, pair_rows
-            self.own_columns, self.pair_columns = own_columns, pair_columns
+        def __init__(self, name, by_col=False, ends=None):
+            self.name, self.by_col, self.ends = name, by_col, ends
             self.stage, self.land, self.got = r["st_" + name], r["land_" + name], r["got_" + name]
-            self.count, self.depth = flows_of(z)[name][:2]
+            self.count, self.depth, self.each = flows_of(z)[name]
             self.send = take("send", 2 * line)
             self.recv = take("recv", 2 * (line + 2))
-            self.local = take("local", 1)
-            self.later = False
+            self.local = take("local", 2)
+            self.done = False
 
         def half(self, group):
             return jnp.where(col == 0, group, 1 - group) if self.by_col else group
+
+        def staged(self, chunk, half, tiles=slice(None)):
+            return self.stage.at[chunk, half, tiles, :, : self.each]
 
         def copy(self, chunk, group, slot, device):
             half = self.half(group)
             return remote(
-                self.stage.at[chunk, half],
+                self.staged(chunk, half),
                 self.land.at[slot, half],
                 self.send + 2 * chunk + group,
                 self.recv + 2 * slot + group,
                 device,
             )
 
-        def sums(self, chunk):
-            own, pair = turned(self.own_rows[chunk]), turned(self.pair_rows[chunk])
-
-            def tile_sums(group, tile):
-                at = slice(tile * self.depth, (tile + 1) * self.depth) if self.split else slice(None)
-                column = 0 if self.split else tile
-                part = contract(own[at], self.own_columns(group, column), 1, 0)
-                return part + contract(pair[at], self.pair_columns(group, column), 1, 0)
-
-            return tile_sums
-
-        def add(self, rank, chunk, slot, device):
-            tile_sums = self.sums(chunk)
-            self.free(chunk, device)
+        def keep(self, chunk, group, tile, value):
+            self.stage[chunk, self.half(group), tile, :, : self.each] = value.astype(bf16)
+
+        def add(self, chunk, group, slot, device):
+            half = self.half(group)
+            self.copy(chunk, group, slot, device).wait_recv()
+            got = self.got.at[:, :, : self.each]
+            bring = local(self.land.at[slot, half], got, self.local)
+            bring.start()
+            bring.wait()
+            for tile in range(self.count):
+                whole = self.stage[chunk, half, tile, :, : self.each].astype(f32) + got[tile].astype(f32)
+                self.keep(chunk, group, tile, whole)
+
+        def out_from_end(self, number, tile=None):
+            @pl.when(at_end)
+            def _():
+                chunk = counted(line - 1 - number)
+                slot = chunk if number < line - 2 else jnp.where(first_half, line, line + 1)
+                for group in range(2):
+                    half = self.half(group)
+                    if tile is None:
+                        self.copy(chunk, group, slot, inward).start()
+                    else:
+                        remote(
+                            self.staged(chunk, half, tile),
+                            self.land.at[slot, half, tile],
+                            self.send + 2 * chunk + group,
+                            self.recv + 2 * slot + group,
+                            inward,
+                        ).start()
+
+        def to_mate(self, number):
+            @pl.when(near_end)
+            def _():
+                chunk = counted(line - 1 - number)
+                slot = chunk if number == 0 else jnp.where(first_half, line, line + 1)
+                if self.ends is not None:
+                    self.product(chunk, True)
+                for group in range(2):
+                    if self.ends is None:
+                        self.add(chunk, group, chunk, outward)
+                    self.copy(chunk, group, slot, mate).start()
+
+        def to_end(self):
+            @pl.when(near_end)
+            def _():
+                chunk = counted(0)
+                slot = jnp.where(first_half, line + 1, line)
+                if self.ends is not None:
+                    self.product(chunk, False)
+                for group in range(2):
+                    self.add(chunk, group, chunk, mate)
+                    self.copy(chunk, group, slot, outward).start()
+
+        def own(self):
             if self.ends is not None:
 
-                @pl.when(rank == 1)
+                @pl.when(at_end)
                 def _():
-                    self.bring_end(chunk)
-
+                    self.product(place, False)
+
+                @pl.when(near_end)
+                def _():
+                    self.product(place, True)
+
+            self.out = local(self.staged(place, slice(None)), r["own_" + self.name], self.local + 1)
+            self.out.start()
+
+        def sent(self):
+            self.done = True
+            self.out.wait()
+
+            def one(chunk):
+                for group in range(2):
+                    self.copy(chunk, group, chunk, inward).wait_send()
+
+            if self.ends is None:
+
+                @pl.when(at_end)
+                def _():
+                    for number in range(line - 1):
+                        one(counted(line - 1 - number))
+
+            @pl.when(near_end)
+            def _():
+                for chunk in (line - 1, line - 2, 0):
+                    one(counted(chunk))
+
+        def finish(self):
+            if not self.done:
+                self.sent()
+            far = 0 if self.ends is None else 1
             for group in range(2):
-                half = self.half(group)
-
-                @pl.when(rank > (0 if self.ends is None else 1))
+
+                @pl.when(place > far)
                 def _():
-                    self.copy(chunk, group, chunk, device).wait_recv()
-                    bring = local(self.land.at[chunk, half], self.got, self.local)
-                    bring.start()
-                    bring.wait()
-
-                if self.ends is None:
-
-                    @pl.when(rank == 0)
-                    def _():
-                        self.got[...] = jnp.zeros_like(self.got)
-
-                else:
-
-                    @pl.when(rank == 1)
-                    def _():
-                        self.end_sums(group)
-
+                    self.copy(place, group, line, left).wait_recv()
+
+                @pl.when(place < line - 1 - far)
+                def _():
+                    self.copy(place, group, line + 1, right).wait_recv()
+
+    class ColumnFlow(Flow):
+        def __init__(self, name, own, pair):
+            super().__init__(name, by_col=True)
+            self.own_columns, self.pair_columns = own, pair
+
+        def products(self, tile):
+            for group in range(2):
+                full = contract(r["hid_own"][...], r[self.own_columns[group]][tile], 0, 0)
+                full = full + contract(r["hid_pair"][...], r[self.pair_columns[group]][tile], 0, 0)
+                for chunk in range(line):
+                    self.keep(chunk, group, tile, full[chunk * self.depth : (chunk + 1) * self.depth])
+
+    class RowFlow(Flow):
+        def __init__(self, name, own, pair, ends):
+            super().__init__(name, ends=ends)
+            self.own_rows, self.pair_rows = own, pair
+
+        def product(self, chunk, with_end):
+            copies = self.bring_end(chunk) if with_end else []
+            for copy in copies:
+                copy.start()
+            for group in range(2):
+                full = contract(self.own_rows[chunk], r["cotq"][0, group], 0, 0)
+                full = full + contract(self.pair_rows[chunk], r["cotp"][group], 0, 0)
+                for copy in copies:
+                    copy.wait()
+                copies = []
+                if with_end:
+                    for pair in range(2):
+                        rows_in = r["weight"][1, pair, :rows, : self.count * self.depth]
+                        cot_in = r["weight"][0, pair, group * rows : (group + 1) * rows, :q]
+                        full = full + contract(rows_in, cot_in, 0, 0)
                 for tile in range(self.count):
-                    whole = tile_sums(group, tile) + self.got[tile].astype(f32)
-                    self.stage[chunk, half, tile] = whole.astype(bf16)
-                self.copy(chunk, group, slot, device).start()
-
-        def free(self, chunk, device):
-            if self.earlier is not None:
-
-                @pl.when(jnp.logical_not(at_end))
-                def _():
-                    for group in range(2):
-                        self.earlier.copy(chunk, group, chunk, device).wait_send()
+                    self.keep(chunk, group, tile, full[tile * self.depth : (tile + 1) * self.depth])
 
         def bring_end(self, chunk):
-            self.ends.bring(chunk)
             copies = []
+            self.ends.onward(chunk).wait_recv()
             for pair in range(2):
                 rows_in = self.ends.land.at[chunk, pair]
                 copies.append(local(rows_in, r["weight"].at[1, pair, :rows, : rows_in.shape[1]], stream_base + pair))
                 for part in range(2):
                     at = r["weight"].at[0, pair, part * rows : (part + 1) * rows, :q]
                     copies.append(local(r["end_cot"].at[pair, part], at, stream_base + 2 + 2 * pair + part))
-            for copy in copies:
-                copy.start()
-            for copy in copies:
-                copy.wait()
-
-        def end_sums(self, group):
-            columns = self.depth * self.count if self.split else self.depth
-            for tile in range(self.count):
-                at = slice(tile * self.depth, (tile + 1) * self.depth)
-                total = None
-                for pair in range(2):
-                    left = turned(r["weight"][1, pair, :rows, :columns][:, at])
-                    part = contract(left, r["weight"][0, pair, group * rows : (group + 1) * rows, :q], 1, 0)
-                    total = part if total is None else total + part
-                self.got[tile] = total.astype(bf16)
-
-        def start(self, tile):
-            for way, end, device in ((0, 0, right), (1, line - 1, left)):
-
-                @pl.when(place == end)
-                def _():
-                    chunk = (line - 1) * (1 - way)
-                    if tile == 0:
-                        self.free(chunk, device)
-                    tile_sums = self.sums(chunk)
-                    for group in range(2):
-                        half = self.half(group)
-                        self.stage[chunk, half, tile] = tile_sums(group, tile).astype(bf16)
-                        remote(
-                            self.stage.at[chunk, half, tile],
-                            self.land.at[chunk, half, tile],
-                            self.send + 2 * chunk + group,
-                            self.recv + 2 * chunk + group,
-                            device,
-                        ).start()
-
-        def step(self, number):
-            def one(way, carry):
-                rightward = way == 0
-                rank = jnp.where(rightward, place, line - 1 - place)
-                chunk = jnp.where(rightward, line - 1 - number + place, place - (line - 1) + number)
-                slot = jnp.where(chunk == place + 1 - 2 * way, line + way, chunk)
-                device = {"dp": dp + 2 - 4 * way}
-
-                @pl.when((rank <= number) & (rank < line - 1) & (rank >= (0 if self.ends is None else 1)))
-                def _():
-                    self.add(rank, chunk, slot, device)
-
-                return carry
-
-            lax.fori_loop(0, 2, one, 0)
-
-        def steps(self, first, last):
-            if last - first == 1:
-                self.step(first)
-            elif last > first:
-                loop(first, last, self.step)
-
-        def own(self):
-            if self.earlier is not None:
-                self.earlier.out.wait()
-                self.earlier.later = True
-            tile_sums = self.sums(place)
-            if self.ends is not None:
-
-                @pl.when(near_end)
-                def _():
-                    self.bring_end(place)
-
-            for group in range(2):
-                if self.ends is not None:
-
-                    @pl.when(near_end)
-                    def _():
-                        self.end_sums(group)
-
-                    @pl.when(jnp.logical_not(near_end))
-                    def _():
-                        self.got[...] = jnp.zeros_like(self.got)
-
-                for tile in range(self.count):
-                    whole = tile_sums(group, tile)
-                    if self.ends is not None:
-                        whole = whole + self.got[tile].astype(f32)
-                    self.stage[place, self.half(group), tile] = whole.astype(bf16)
-            self.out = local(self.stage.at[place], r["own_" + self.name], self.local)
-            self.out.start()
-
-        def finish(self):
-            if not self.later:
-                self.out.wait()
-            far = 0 if self.ends is None else 1
-            for group in range(2):
-
-                @pl.when(place > far)
-                def _():
-                    self.copy(place, group, line, left).wait_recv()
-
-                @pl.when(place < line - 1 - far)
-                def _():
-                    self.copy(place, group, line + 1, right).wait_recv()
-
-            def sent(chunk):
-                @pl.when((chunk != place) & (jnp.logical_not(at_end) if far else True))
-                def _():
-                    for group in range(2):
-                        self.copy(chunk, group, chunk, right).wait_send()
-
-            if not self.later:
-                loop(0, line, sent)
-
-    cot_own_tile = lambda group, tile: r["cotq"][0, group]
-    cot_pair_tile = lambda group, tile: r["cotp"][group]
-    down = Flow("down", r["act_own"], r["act_pair"], cot_own_tile, cot_pair_tile, split=True, ends=end_act)
-    up = Flow(
-        "up",
-        r["hid_own"],
-        r["hid_pair"],
-        lambda group, tile: r[("db_mine", "db_theirs")[group]][tile],
-        lambda group, tile: r[("db_mine_pair", "db_theirs_pair")[group]][tile],
-        by_col=True,
-        earlier=down if shared else None,
-    )
-    dense = Flow("dense", r["att_own"], r["att_pair"], cot_own_tile, cot_pair_tile, ends=end_att)
-    qkv = Flow(
-        "qkv",
-        r["hid_own"],
-        r["hid_pair"],
-        lambda group, tile: r[("dp_mine", "dp_theirs")[group]][tile],
-        lambda group, tile: r[("dp_mine_pair", "dp_theirs_pair")[group]][tile],
-        by_col=True,
-    )
-    cuts = (0, 1, line // 2, line - 1)
-
+            return copies
+
+    down = RowFlow("down", r["act_own"], r["act_pair"], end_act)
+    up = ColumnFlow("up", ("db_mine", "db_theirs"), ("db_mine_pair", "db_theirs_pair"))
+    dense = RowFlow("dense", r["att_own"], r["att_pair"], end_att)
+    qkv = ColumnFlow("qkv", ("dp_mine", "dp_theirs"), ("dp_mine_pair", "dp_theirs_pair"))
     swaps["qkv"].wait()
 
     def qkv_work(step, slot):
@@ -880,6 +846,8 @@
     loop(0, 1, pass_on(act_side, act_on))
     loop(0, 1, waits(act_on))
     end_act.start(True, 0, 1)
+    cot_side_onward.wait()
+    send_end_cot(1, other_row)
 
     att_side_send, att_side_recv = take("send", half_line), take("recv", half_line)
     att_col_send, att_col_recv = take("send", half_line), take("recv", half_line)
@@ -925,14 +893,6 @@
                 r["att_part"][chunk] = piece
                 att_side(k).start()
 
-    loop(0, pairs // 2, head_pair)
-    cot_side_onward.wait()
-    send_end_cot(1, other_row)
-    loop(1, half_line, pass_on(act_side, act_on))
-    loop(1, half_line, waits(act_on))
-    end_act.start(True, 1, line - 1)
-    loop(pairs // 2, pairs, head_pair)
-
     def near_end_cot():
         @pl.when(near_end)
         def _():
@@ -940,8 +900,24 @@
                 for part in range(2):
                     end_cot(pair, part, outward).wait_recv()
 
-    near_end_cot()
-    down.steps(cuts[1], cuts[2])
+    def pair_and_more(pair):
+        head_pair(pair)
+
+        @pl.when(pair == 0)
+        def _():
+            loop(1, half_line, pass_on(act_side, act_on))
+            loop(1, half_line, waits(act_on))
+            end_act.start(True, 1, line - 1)
+            end_act.hand_over(0)
+
+        @pl.when(pair == 1)
+        def _():
+            near_end_cot()
+            down.to_mate(0)
+            end_act.hand_over(1, 2)
+
+    loop(0, pairs, pair_and_more)
+    down.to_mate(1)
 
     def scatter(name, total, earlier=None):
         across = Message(r["part_send"], r[name + "_got"], to_col)
@@ -966,10 +942,11 @@
                 total[p] = total[p] + r[name + "_got"][p].astype(f32)
             r["part_row"][...] = total[other_row].astype(bf16)
             over.start()
-
-        def third():
+            return total[row]
+
+        def third(part):
             over.wait()
-            return total[row] + r[name + "_row"][...].astype(f32)
+            return part + r[name + "_row"][...].astype(f32)
 
         return first, second, third, (across, over)
 
@@ -1013,21 +990,33 @@
                 part = contract(r["dp_mine"][step], r["weight"][slot, h, p * q : (p + 1) * q, :PAIR_QKV], 1, 1)
                 total[2 * h + p] = total[2 * h + p] + part
 
+    def take_d_before(tile):
+        loop(tile, tile + 1, pass_on(db_side, db_on))
+        loop(tile, tile + 1, waits(db_col, db_on))
+        up.products(tile)
+        up.out_from_end(0, tile)
+        up.out_from_end(1, tile)
+
+    hid_side.wait()
+    take_d_before(0)
     stream(tiles, column_tiles("up", z.down_chunk), up_back)
+    take_d_before(1)
     stream(pairs, column_tiles("qkv", PAIR_QKV), qkv_back)
     dh_first, dh_second, dh_third, dh_messages = scatter("dh", total)
     dh_first()
-    hid_side.wait()
-    for tile in range(tiles):
-        loop(tile, tile + 1, pass_on(db_side, db_on))
-        loop(tile, tile + 1, waits(db_col, db_on))
-        up.start(tile)
-        if tile == tiles // 2:
-            down.steps(cuts[2], cuts[3])
-    dh_second()
-    up.steps(cuts[1], cuts[2])
-
-    d_hidden = dh_third()
+    for tile in range(2, tiles):
+        take_d_before(tile)
+    up.out_from_end(2)
+    down.to_end()
+    r["grad_inputs"][...] = dh_second()
+    up.to_mate(0)
+    up.to_mate(1)
+    stream(tiles, row_tiles("down", z.down_chunk), down_out)
+    stream(1, row_tiles("dense", z.features), dense_out)
+    out_first, out_second, out_third, out_messages = scatter("out", total, dh_messages)
+    out_first()
+
+    d_hidden = dh_third(r["grad_inputs"][...])
     r["grad_inputs"][...] = d_hidden
     own_in = r["inq"].at[0, row]
     gain = r["gainq"][0, row, 0:1, :]
@@ -1047,15 +1036,67 @@
     small_side = Message(r["sums"], r["sums_got"].at[0], to_side)
     small_side.start()
 
-    stream(tiles, row_tiles("down", z.down_chunk), down_out)
-    stream(1, row_tiles("dense", z.features), dense_out)
-    out_first, out_second, out_third, out_messages = scatter("out", total, dh_messages)
-    out_first()
+    small_send, small_recv = take("send", 2), take("recv", 2)
+
+    def small(way, device):
+        return remote(r["sums_send"].at[way], r["sums_got"].at[1 + way], small_send + way, small_recv + way, device)
+
+    def hop(number):
+        for way, rank, device, last in ((0, place, right, has_right), (1, line - 1 - place, left, has_left)):
+
+            @pl.when((rank == number) & last)
+            def _():
+                @pl.when(rank == 0)
+                def _():
+                    r["sums_send"][way] = r["sums"][...]
+
+                @pl.when(rank > 0)
+                def _():
+                    small(way, device).wait_recv()
+                    r["sums_send"][way] = r["sums"][...] + r["sums_got"][1 + way]
+
+                small(way, device).start()
+
+    branch = out_second()
+    total[0] = branch
+    down.own()
+    down.sent()
+    for pair in range(pairs):
+        loop(pair, pair + 1, pass_on(dp_side, dp_on))
+        loop(pair, pair + 1, waits(dp_col, dp_on))
+        qkv.products(pair)
+    loop(0, half_line, pass_on(att_side, att_on))
+    loop(0, half_line, waits(att_col, att_on))
+    end_att.start(False, 0, line - 1)
+    end_att.start(True, 0, line - 1)
+    small_side.wait()
+    small_side.copy().wait_send()
+    pending.remove(small_side)
+    r["sums"][...] = r["sums"][...] + r["sums_got"][0]
+    hop(0)
+    for number in range(line - 1):
+        qkv.out_from_end(number)
+    up.to_end()
+    hop(1)
     sums_row.wait()
     r["sum_send"][1] = r["sum_send"][0] + r["sum_got"][0]
     sums_col.start()
-    up.steps(cuts[2], cuts[3])
-    out_second()
+    up.own()
+    end_att.hand_over(0, 1, 2)
+    dense.to_mate(0)
+    dense.to_mate(1)
+    hop(2)
+    qkv.to_mate(0)
+    dense.to_end()
+    qkv.to_mate(1)
+    qkv.to_end()
+    qkv.own()
+
+    dense.own()
+    branch = out_third(total[0])
+    bias = as_row(r["out_bias"][...])
+    valid = (r["seg_col"][...] < z.seqs).astype(f32)
+    r["outputs"][...] = (r["inq"][0, row].astype(f32) + valid * (branch + bias)).astype(bf16)
     sums_col.wait()
     both = r["sum_send"][1] + r["sum_got"][1]
     spread = turned(jnp.concatenate([both, jnp.zeros((120, rows), f32)], axis=0))
@@ -1064,60 +1105,6 @@
     d_normed = r["grad_inputs"][...] * gain
     r["grad_inputs"][...] = cot[...].astype(f32) + r["stat"][1] * (d_normed - part_one - normed * part_two)
 
-    small_send, small_recv = take("send", 2), take("recv", 2)
-
-    def small(way, device):
-        return remote(r["sums_send"].at[way], r["sums_got"].at[1 + way], small_send + way, small_recv + way, device)
-
-    def hop(number):
-        for way, rank, device, last in ((0, place, right, has_right), (1, line - 1 - place, left, has_left)):
-
-            @pl.when((rank == number) & last)
-            def _():
-                @pl.when(rank == 0)
-                def _():
-                    r["sums_send"][way] = r["sums"][...]
-
-                @pl.when(rank > 0)
-                def _():
-                    small(way, device).wait_recv()
-                    r["sums_send"][way] = r["sums"][...] + r["sums_got"][1 + way]
-
-                small(way, device).start()
-
-    def hops(first, last):
-        if last - first == 1:
-            hop(first)
-        elif last > first:
-            loop(first, last, hop)
-
-    loop(0, pairs, pass_on(dp_side, dp_on))
-    loop(0, half_line, pass_on(att_side, att_on))
-    loop(0, half_line, waits(att_col, att_on))
-    end_att.start(False, 0, line - 1)
-    end_att.start(True, 0, line - 1)
-    loop(0, pairs, waits(dp_col, dp_on))
-    qkv.steps(cuts[0], cuts[1])
-    branch = out_third()
-    bias = as_row(r["out_bias"][...])
-    valid = (r["seg_col"][...] < z.seqs).astype(f32)
-    r["outputs"][...] = (r["inq"][0, row].astype(f32) + valid * (branch + bias)).astype(bf16)
-    small_side.wait()
-    small_side.copy().wait_send()
-    pending.remove(small_side)
-    r["sums"][...] = r["sums"][...] + r["sums_got"][0]
-    hops(cuts[0], cuts[1])
-    down.own()
-    dense.steps(cuts[1], cuts[2])
-    qkv.steps(cuts[1], cuts[2])
-    hops(cuts[1], cuts[2])
-    up.own()
-    dense.steps(cuts[2], cuts[3])
-    qkv.steps(cuts[2], cuts[3])
-    hops(cuts[2], cuts[3])
-    dense.own()
-    qkv.own()
-
     r["small"][...] = r["sums"][...]
 
     @pl.when(place == line - 1)
@@ -1168,7 +1155,7 @@
     loop(0, half_line, sent(act_side, act_col, act_on, att_side, att_col, att_on))
     loop(0, tiles, sent(db_side, db_col, db_on))
     loop(0, pairs, sent(dp_side, dp_col, dp_on))
-    assert marks["send"] <= SENDS * line and marks["recv"] <= SENDS * line and marks["local"] <= 16
+    assert marks["send"] <= SENDS * line and marks["recv"] <= SENDS * line and marks["local"] <= LOCALS
 
 
 def on_device(
@@ -1247,7 +1234,7 @@
         out_specs=[pl.BlockSpec(memory_space=space) for shape, kind, space in results.values()],
         out_shape=[jax.ShapeDtypeStruct(shape, kind) for shape, kind, space in results.values()],
         scratch_shapes=[pltpu.VMEM(shape, kind) for shape, kind in scratch.values()]
-        + [pltpu.SemaphoreType.DMA((SENDS * line,)), pltpu.SemaphoreType.DMA((SENDS * line,)), pltpu.SemaphoreType.DMA((16,))],
+        + [pltpu.SemaphoreType.DMA((SENDS * line,)), pltpu.SemaphoreType.DMA((SENDS * line,)), pltpu.SemaphoreType.DMA((LOCALS,))],
         compiler_params=pltpu.CompilerParams(
             collective_id=0, has_side_effects=True, vmem_limit_bytes=VMEM_LIMIT
         ),

time: 265 us -> 253 us (0.955)
  Pallas kernels: 260 us -> 248 us
    pallas_call x1, Pallas kernels: 249 us -> 238 us  [on_device(): pl.pallas_call(partial(layer_kernel, z, names), in_specs=[pl.BlockSpec(me...]
where the time goes in v1:
time: 253 us; the launch traced here: 249 us
  Pallas kernels  248 us (98%)
    pallas_call x1, Pallas kernels, on_device(): pl.pallas_call(partial(layer_kernel, z, names), in_specs=[pl.BlockSpec(me...  238 us
    pallas_call x1, Pallas kernels, finish(): pl.pallas_call(kernel, grid=(steps,), in_specs=in_specs, out_specs=out_sp...  10.2 us

profile of v1, /device:TPU:9, one launch (start us, length us, event | category | flops | bytes accessed | tf_op | source)
XLA Modules:
  0.0 249.1 jit_solution(12219566152025941573)
XLA Ops:
  0.6 237.9 %layer.1 = (bf16[512,512]{1,0:T(8,128)(2,1)}, f32[512,512]{1,0:T(8,128)}, f32[1,5120]{1,0:T(1,128)}, bf16[1024,2048]{1,0:T(8,128)(2,1)}, bf16[2048,1024]{1,0:T(8...) custom-call(bf16[512,512]{1,0:T(8,128)(2,1)} %refs_0_.1, ...), custom_call_target="tpu_custom_call" | custom-call | tf_op jit(solution)/shard_map/layer/pallas_call | solution.py:1231
  238.5 10.2 %finish.1 = (f32[512,1024]{1,0:T(8,128)}, f32[128,4096]{1,0:T(8,128)}, f32[128,1024]{1,0:T(8,128)}, f32[128,3072]{1,0:T(8,128)}, bf16[512,512]{1,0:T(8,128)(2,1)...) custom-call(bf16[2,4,128,512]{3,2,1,0:T(8,128)(2,1)} %get-tuple-elem, ...), custom_call_target="tpu_custom_call" | custom-call | tf_op jit(solution)/shard_map/finish/pallas_call | solution.py:1322
